TPU v7x, 32 devices: a whole 2x2x4 slice. The times are simulated.
32 devices in a mesh: train: 4 (over y, x), roll: 8 (over z, core).
Axes of the slice: x: 2, y: 2, z: 4, core: 2. Of those that a mesh axis runs over, the one named last changes fastest.
Arguments:
- master_gate: float32 [4, 2048, 7168], P(None, 'roll', 'train'), may hold values from -1 to 1
- master_up: float32 [4, 2048, 7168], P(None, 'roll', 'train'), may hold values from -1 to 1
- master_down: float32 [4, 2048, 7168], P(None, 'roll', 'train'), may hold values from -1 to 1
- tokens: bfloat16 [512, 7168], P('roll'), may hold values from -6 to 6
- expert_ids: int32 [512, 2], P('roll'), may hold values from 0 to 3, all different within a row; in each aligned block of 64 rows (0 to 63, 64 to 127, ...) at most 32 rows name the same one
- gate_weights: float32 [512, 2], P('roll'), may hold values from 0.2 to 1
- placement: int32 [8], replicated, may hold values from 0 to 3, as said below
Outputs:
- slot_gate: bfloat16 [8, 16, 128, 7168], P('roll', None, 'train')
- slot_up: bfloat16 [8, 16, 128, 7168], P('roll', None, 'train')
- slot_down: bfloat16 [8, 16, 128, 7168], P('roll', None, 'train')
- mixed_out: bfloat16 [512, 7168], P('roll', 'train')
Inputs may be any that keep to these rules, and one draw needn't show every extreme that they name: `expert_ids`: the 2 experts of a row differ. In each aligned block of 64 rows (the rows of one index of roll) no expert is named by more than 32 rows, a bound that some block reaches. `placement`: every expert of the window is held by exactly two owners.
All inputs are finite; a program needn't handle non-finite values. Where the computation divides by a largest or mean magnitude, that divisor is 1e-20 or more.
Results may differ from a plain program's by a relative error of at most 0.0093.
Values may be sent and summed in bfloat16 or wider, within the bound.
No kernel may reach another device: no remote copies, remote signals or barrier semaphores. Data moves between devices by JAX's collectives and lax.ppermute only.
A program may use at most 256 MiB of HBM per device.

v0:
```python
import functools

import jax
import jax.numpy as jnp
from jax import lax
from jax.experimental import pallas as pl
from jax.experimental.pallas import tpu as pltpu
from jax.sharding import PartitionSpec as P

BLOCK = 128
CORES = 2
VMEM_BYTES = 48 * 1024 * 1024
LIGHT = pl.CostEstimate(flops=1, bytes_accessed=1, transcendentals=0)


def any_spec():
    return pl.BlockSpec(memory_space=pl.ANY)


def smem_spec():
    return pl.BlockSpec(memory_space=pltpu.SMEM)


def quantize_kernel(trains, x_ref, *refs):
    q_ref, d_ref = refs[-2:]
    rows = BLOCK // trains
    features = x_ref.shape[-1]
    for col in range(features // BLOCK):
        cols = slice(col * BLOCK, (col + 1) * BLOCK)
        block = x_ref[0, :, cols]
        peak = jnp.max(jnp.max(jnp.abs(block), axis=0, keepdims=True), axis=1, keepdims=True)
        scale = peak.astype(jnp.bfloat16).astype(jnp.float32)
        quant = (block * (1.0 / scale)).astype(jnp.bfloat16)
        q_ref[:, 0, 0, :, cols] = quant.reshape(trains, rows, BLOCK)
        d_ref[0, 0, :, cols] = (quant.astype(jnp.float32) * scale).astype(jnp.bfloat16)


def quantize(master, first, blocks, trains, slots, base=0, into=None, after=()):
    experts, _, features = master.shape
    rows = BLOCK // trains
    operands = [master] + list(after) + ([] if into is None else [into])
    return pl.pallas_call(
        functools.partial(quantize_kernel, trains),
        grid=(experts, blocks),
        in_specs=[pl.BlockSpec((1, BLOCK, features), lambda e, b: (e, first + b, 0))]
        + [any_spec()] * (len(operands) - 1),
        out_specs=[
            pl.BlockSpec((trains, 1, 1, rows, features), lambda e, b: (0, base + e, b, 0, 0)),
            pl.BlockSpec((1, 1, BLOCK, features), lambda e, b: (e, b, 0, 0)),
        ],
        out_shape=[
            jax.ShapeDtypeStruct((trains, slots, blocks, rows, features), jnp.bfloat16),
            jax.ShapeDtypeStruct((experts, blocks, BLOCK, features), jnp.bfloat16),
        ],
        input_output_aliases={} if into is None else {len(operands) - 1: 0},
        compiler_params=pltpu.CompilerParams(vmem_limit_bytes=VMEM_BYTES),
        cost_estimate=LIGHT,
        name="quantize",
    )(*operands)


def start_choice(plan_ref, arrays, choice, target, sem):
    tests, array, (kind, n, *more) = choice
    ref = arrays[array]
    if kind == "is":
        view = ref.at[n]
    elif kind == "at":
        view = ref.at[plan_ref[n]]
    else:
        view = ref.at[:, plan_ref[n] + more[0], pl.ds(more[1], 1)]
    hit = None
    for place, value in tests:
        test = plan_ref[place] == value
        hit = test if hit is None else hit & test

    def go():
        pltpu.make_async_copy(view, target, sem).start()

    if hit is None:
        go()
    else:
        pl.when(hit)(go)


def pack_kernel(pieces, n_in, plan_ref, *refs):
    arrays = refs[:n_in]
    out, held, sem_in, sem_out = refs[-4:]
    for n, choices in enumerate(pieces):
        for choice in choices:
            start_choice(plan_ref, arrays, choice, held.at[n], sem_in.at[n])
    for n in range(len(pieces)):
        pltpu.make_async_copy(held.at[n], held.at[n], sem_in.at[n]).wait()
        pltpu.make_async_copy(held.at[n], out.at[n], sem_out.at[n]).start()
    for n in range(len(pieces)):
        pltpu.make_async_copy(held.at[n], out.at[n], sem_out.at[n]).wait()


class Arrays:
    def __init__(self):
        self.items = []

    def add(self, array):
        for n, item in enumerate(self.items):
            if item is array:
                return n
        self.items.append(array)
        return len(self.items) - 1


def number_choices(pieces, arrays):
    return [[(tests, arrays.add(a), index) for tests, a, index in choices] for choices in pieces]


def pack(plan, shape, pieces, after=()):
    arrays = Arrays()
    pieces = number_choices(pieces, arrays)
    n_in = len(arrays.items)
    size = len(pieces)
    for dim in shape:
        size *= dim
    operands = arrays.items + list(after)
    return pl.pallas_call(
        functools.partial(pack_kernel, pieces, n_in),
        in_specs=[smem_spec()] + [any_spec()] * len(operands),
        out_specs=any_spec(),
        out_shape=jax.ShapeDtypeStruct((len(pieces),) + shape, jnp.bfloat16),
        scratch_shapes=[
            pltpu.VMEM((len(pieces),) + shape, jnp.bfloat16),
            pltpu.SemaphoreType.DMA((len(pieces),)),
            pltpu.SemaphoreType.DMA((len(pieces),)),
        ],
        compiler_params=pltpu.CompilerParams(vmem_limit_bytes=VMEM_BYTES),
        cost_estimate=LIGHT,
        name="pack",
    )(plan, *operands)


def place_kernel(pieces, sources, first, blocks, n_in, plan_ref, *refs):
    arrays = refs[:n_in]
    out, mark, held, sem_in, sem_out = refs[-5:]
    trains, count, _, features = held.shape[1:]
    for n, choices in enumerate(pieces):
        for choice in choices:
            start_choice(plan_ref, arrays, choice, held.at[n], sem_in.at[n])
    mark[...] = jnp.zeros_like(mark)
    stores = []
    for n in range(len(pieces)):
        pltpu.make_async_copy(held.at[n], held.at[n], sem_in.at[n]).wait()
        start = plan_ref[sources[n]] * blocks + first
        for part in range(trains):
            store = pltpu.make_async_copy(
                held.at[n, part],
                out.at[pl.ds(start, count), :, pl.ds(part * features, features)],
                sem_out.at[n, part],
            )
            store.start()
            stores.append(store)
    for store in stores:
        store.wait()


def place_pieces(plan, shape, owners, pieces, sources, first, blocks, out, after=()):
    trains, count, rows, features = shape
    arrays = Arrays()
    pieces = number_choices(pieces, arrays)
    n_in = len(arrays.items)
    operands = arrays.items + list(after) + ([] if out is None else [out])
    return pl.pallas_call(
        functools.partial(place_kernel, pieces, sources, first, blocks, n_in),
        in_specs=[smem_spec()] + [any_spec()] * len(operands),
        out_specs=[any_spec(), pl.BlockSpec(memory_space=pltpu.VMEM)],
        out_shape=[
            jax.ShapeDtypeStruct((owners * blocks, rows, trains * features), jnp.bfloat16),
            jax.ShapeDtypeStruct((8, BLOCK), jnp.float32),
        ],
        scratch_shapes=[
            pltpu.VMEM((len(pieces),) + shape, jnp.bfloat16),
            pltpu.SemaphoreType.DMA((len(pieces),)),
            pltpu.SemaphoreType.DMA((len(pieces), trains)),
        ],
        input_output_aliases={} if out is None else {len(operands): 0},
        compiler_params=pltpu.CompilerParams(vmem_limit_bytes=VMEM_BYTES),
        cost_estimate=LIGHT,
        name="place_pieces",
    )(plan, *operands)


def plan_places(experts):
    names = [f"send{slot}" for slot in range(experts)]
    names += ["inner", "core", "chip", "side", "own", "mate", "out0", "out1", "most"]
    names += [f"{list_}_{who}" for list_ in ("here", "there") for who in ("own", "mate", "out0", "out1")]
    names += [f"from_{who}{n}" for who in ("own", "mate") for n in range(4)]
    return {name: n for n, name in enumerate(names)}


def plan_kernel(experts, owners, places, me_ref, placement_ref, out_ref):
    me = me_ref[0]
    chip, core = lax.div(me, CORES), lax.rem(me, CORES)
    side = lax.div(chip, 2)
    half = owners // 2
    needs, ranks = [], []
    for s in range(2):
        need = []
        for e in range(experts):
            found = jnp.int32(0)
            for o in range(s * half, (s + 1) * half):
                found = jnp.where(placement_ref[o] == e, 1, found)
            need.append(found)
        rank = []
        for e in range(experts):
            total = jnp.int32(0)
            for other in range(experts):
                if other != e:
                    ahead = need[other] >= need[e] if other < e else need[other] > need[e]
                    total = total + jnp.where(ahead, 1, 0)
            rank.append(total)
        needs.append(sum(need))
        ranks.append(rank)
    here = [jnp.where(side == 0, a, b) for a, b in zip(*ranks)]
    there = [jnp.where(side == 0, b, a) for a, b in zip(*ranks)]
    outer = 3 * side
    values = {
        "inner": jnp.where((chip == 1) | (chip == 2), 1, 0),
        "core": core,
        "chip": chip,
        "side": side,
        "own": placement_ref[me],
        "mate": placement_ref[chip * CORES + 1 - core],
        "out0": placement_ref[outer * CORES],
        "out1": placement_ref[outer * CORES + 1],
        "most": jnp.maximum(*needs),
    }
    for slot in range(experts):
        values[f"send{slot}"] = sum(jnp.where(there[e] == slot, e, 0) for e in range(experts))
    for who in ("own", "mate", "out0", "out1"):
        for list_, rank in (("here", here), ("there", there)):
            values[f"{list_}_{who}"] = sum(
                jnp.where(values[who] == e, rank[e], 0) for e in range(experts)
            )
    for n, source in enumerate((chip, 1 + 4 * side - chip, 2 - side, 3 - 3 * side)):
        values[f"from_own{n}"] = source * CORES + core
        values[f"from_mate{n}"] = source * CORES + 1 - core
    for name, n in places.items():
        out_ref[n] = values[name]


def make_plan(placement, experts, owners, after=()):
    places = plan_places(experts)
    me = jnp.reshape(lax.axis_index("roll"), (1,)).astype(jnp.int32)
    plan = pl.pallas_call(
        lambda *refs: plan_kernel(experts, owners, places, refs[0], refs[1], refs[-1]),
        in_specs=[smem_spec(), smem_spec()] + [any_spec()] * len(after),
        out_specs=smem_spec(),
        out_shape=jax.ShapeDtypeStruct((len(places),), jnp.int32),
        cost_estimate=LIGHT,
        name="plan",
    )(me, placement, *after)
    return plan, places


def line_schedule(opens, experts, cap, ride_from):
    chunks = range(len(opens))
    own, far = list(chunks), list(chunks)
    fresh = [("x", c, i) for c in chunks for i in range(CORES)]
    near = [("near", c, s) for c in chunks for s in range(cap, experts)]
    middle, inwards, outwards = [], [], []
    arrived, relayed, ride_due = [], [], {"in": ride_from}
    n = 0
    while own or arrived or far or near or fresh or relayed or ride_due:
        across, ins, outs = [], [], []
        if arrived and arrived[0][0] <= n:
            c = arrived.pop(0)[1]
            across = [("far", c, s) for s in range(cap)]
        elif own and opens[own[0]] <= n:
            c = own.pop(0)
            across = [("own", c, s) for s in range(cap)]
        if across:
            relayed += [(n + 2, (across[0][0], c, i)) for i in range(CORES)]
        if ride_due.get("across", n + 1) <= n and (not across or across[0][0] == "own"):
            across.append(("ride", 0, 0))
            del ride_due["across"]
            ride_due["out"] = n + 2
        if far and opens[far[0]] <= n:
            c = far.pop(0)
            ins = [("far", c, s) for s in range(cap)]
            arrived.append((n + 2, c))
        else:
            if ride_due.get("in", n + 1) <= n:
                ins = [("ride", 0, 0), ("ride", 0, 1)]
                del ride_due["in"]
                ride_due["across"] = n + 2
            while near and opens[near[0][1]] <= n and len(ins) < cap:
                ins.append(near.pop(0))
        while relayed and relayed[0][0] <= n and len(outs) < cap:
            outs.append(relayed.pop(0)[1])
        if ride_due.get("out", n + 1) <= n and len(outs) < cap:
            outs.append(("ride", 0, 0))
            del ride_due["out"]
        while fresh and opens[fresh[0][1]] <= n and len(outs) < cap:
            outs.append(fresh.pop(0))
        middle.append(across)
        inwards.append(ins)
        outwards.append(outs)
        n += 1
    return middle, inwards, outwards


def link_pairs(chip_pairs, swap_chips=()):
    pairs = []
    for core in range(CORES):
        for a, b in chip_pairs:
            pairs.append((a * CORES + core, b * CORES + core))
        for chip in swap_chips:
            pairs.append((chip * CORES + core, chip * CORES + 1 - core))
    return pairs


EDGES = ((0, 1), (1, 0), (2, 3), (3, 2))


def line_exchange(x_first, quants, dequant, plan, places, routed, shapes, cap):
    experts, blocks, trains, owners = shapes
    features = x_first.shape[-1]
    rows = BLOCK // trains
    shape = (trains, 1, rows, features)
    chunks = [(m, b) for m in range(3) for b in range(blocks)]
    count = len(chunks)
    opens = [0 if c == 0 else 1 if m == 0 else 4 for c, (m, _) in enumerate(chunks)]
    ride_from = 8
    middle, inwards, outwards = line_schedule(opens, experts, cap, ride_from)
    rounds = len(outwards)
    edge_pairs = link_pairs(EDGES)
    middle_pairs = link_pairs([(1, 2), (2, 1)], swap_chips=(0, 3))
    swap_pairs = link_pairs([], swap_chips=range(4))
    is_inner, is_outer = (places["inner"], 1), (places["inner"], 0)
    on_core = [(places["core"], core) for core in range(CORES)]
    got_edge, got_middle, where = {}, {}, {}
    last = [x_first]

    xs = [x_first] + [
        lax.all_to_all(quant, "train", split_axis=0, concat_axis=0, tiled=True) for quant in quants
    ]

    def local(c, name):
        m, b = chunks[c]
        if c == 0:
            return xs[0], ("expert", places[name], 0, 0)
        if m == 0:
            return xs[1], ("expert", places[name], 0, b - 1)
        return xs[-1], ("expert", places[name], (m - 1) * experts, b)

    def packed(pieces, after=()):
        last[0] = pack(plan, shape, pieces, [last[0]] + list(after))
        return last[0]

    ready = {(c, 0): opens[c] for c in range(count)}

    def note(c, position, n):
        ready[c, position] = max(ready.get((c, position), 0), n)

    from_kind = {"x": 1, "own": 2, "far": 3}
    kind_of = {position: kind for kind, position in from_kind.items()}
    for n in range(rounds):
        for i, piece in enumerate(middle[n]):
            where[("across",) + piece] = (n, i)
            if piece[0] != "ride":
                note(piece[1], 2 if piece[0] == "own" else 3, n)
        for i, piece in enumerate(inwards[n]):
            where[("in",) + piece] = (n, i)
            if piece[0] != "ride":
                note(piece[1], 1, n)
        for i, piece in enumerate(outwards[n]):
            where[("out",) + piece] = (n, i)
            if piece[0] != "ride":
                note(piece[1], from_kind[piece[0]], n)

    def across(kind, c):
        return got_middle[where["across", kind, c, 0][0]]

    def find(c, position, who):
        if position == 0:
            return [((),) + local(c, who)]
        choices = []
        if position == 1:
            for slot in range(experts):
                n, i = where["in", "far" if slot < cap else "near", c, slot]
                test = (places[f"there_{who}"], slot)
                choices.append(((is_inner, test), got_edge[n], ("is", i)))
        else:
            got = across(kind_of[position], c)
            choices.append(((is_inner,), got, ("at", places[f"here_{who}"])))
        for core in range(CORES):
            n, i = where["out", kind_of[position], c, core if who == "own" else 1 - core]
            choices.append(((is_outer, on_core[core]), got_edge[n], ("is", i)))
        return choices

    groups = []
    for c in range(count):
        early = [p for p in range(4) if ready[c, p] < rounds - 4]
        late = [p for p in range(4) if p not in early]
        for positions in (early[:2], early[2:], late):
            if positions:
                groups.append((max(ready[c, p] for p in positions), c, positions))
    groups.sort(key=lambda group: group[0])
    swapped, swap_round, outs = {}, {}, [None, None, None]

    def swap(group, n):
        _, c, positions = group
        pieces = [find(c, p, "mate") for p in positions]
        swap_round[c, positions[0]] = n
        swapped[c, positions[0]] = lax.ppermute(packed(pieces), "roll", swap_pairs)

    def place(group):
        _, c, positions = group
        m, b = chunks[c]
        got = swapped[c, positions[0]]
        pieces = [find(c, p, "own") for p in positions]
        pieces += [[((), got, ("is", n))] for n in range(len(positions))]
        sources = [places[f"from_own{p}"] for p in positions]
        sources += [places[f"from_mate{p}"] for p in positions]
        outs[m], last[0] = place_pieces(
            plan, shape, owners, pieces, sources, b, blocks, outs[m], (last[0],)
        )

    ride = {}
    tokens, ids, weights = routed
    ups, down = dequant[:-1], dequant[-1]

    def ride_first():
        pre, columns = None, 2 * blocks
        for restored in ups:
            for b in range(restored.shape[1]):
                column = 0 if pre is None else column + 1
                pre = pre_activations(tokens, ids, restored, b, pre, column, columns, (last[0],))
                last[0] = pre
        ride["pre"] = lax.psum(pre, "train")
    def ride_mix():
        ride["keep"], going = mix_experts(
            ride["pre"], ids, weights, down, plan, places, (last[0],)
        )
        last[0] = ride["keep"]
        going = going.reshape((-1,) + shape)
        ride["swapped"] = lax.ppermute(going, "roll", swap_pairs)

    def ride_cores():
        got = ride["swapped"].reshape(-1, features)
        ride["sums"], going = sum_cores(plan, places, ride["keep"], got, (last[0],))
        last[0] = ride["sums"]
        ride["in"] = going.reshape((-1,) + shape)

    def ride_in():
        n, i = where["in", "ride", 0, 0]
        got = got_edge[n].reshape(-1, BLOCK, features)
        ride["inner"], going = sum_inwards(plan, places, ride["sums"], got, i, (last[0],))
        last[0] = ride["inner"]
        ride["across"] = going.reshape((-1,) + shape)

    def ride_across():
        n, i = where["across", "ride", 0, 0]
        got = got_middle[n].reshape(-1, BLOCK, features)
        ride["final"], going = sum_across(
            plan, places, ride["sums"], ride["inner"], got, i, (last[0],)
        )
        last[0] = ride["final"]
        ride["out"] = going.reshape((-1,) + shape)

    def ride_out():
        n, i = where["out", "ride", 0, 0]
        got = got_edge[n].reshape(-1, BLOCK, features)
        ride["mixed"] = sum_outwards(
            plan, places, ride["sums"], ride["final"], got, i, (last[0],)
        )
        last[0] = ride["mixed"]

    to_swap, to_place = list(groups), []
    spare = local(0, "own")
    for n in range(rounds):
        while to_swap and to_swap[0][0] <= n - 2:
            to_place.append(to_swap.pop(0))
            swap(to_place[-1], n)
        if middle[n]:
            if where.get(("across", "ride", 0, 0), (-1,))[0] == n:
                ride_in()
            pieces = []
            for kind, c, slot in middle[n]:
                if kind == "own":
                    pieces.append([((),) + local(c, f"send{slot}")])
                elif kind == "ride":
                    pieces.append([((), ride["across"], ("is", 0))])
                else:
                    m, i = where["in", kind, c, slot]
                    pieces.append([((), got_edge[m], ("is", i))])
            after = [got_middle[n - 2]] if n - 2 in got_middle else []
            got_middle[n] = lax.ppermute(packed(pieces, after), "roll", middle_pairs)
        if where["out", "ride", 0, 0][0] == n:
            ride_across()
        pieces = []
        for i in range(max(len(inwards[n]), len(outwards[n]))):
            choices = [((is_inner,),) + spare, ((is_outer,),) + spare]
            if i < len(outwards[n]):
                kind, c, core = outwards[n][i]
                if kind == "x":
                    choices[0] = ((is_inner,),) + local(c, f"out{core}")
                elif kind == "ride":
                    choices[0] = ((is_inner,), ride["out"], ("is", 0))
                else:
                    index = ("at", places[f"here_out{core}"])
                    choices[0] = ((is_inner,), across(kind, c), index)
            if i < len(inwards[n]):
                kind, c, slot = inwards[n][i]
                if kind == "ride":
                    choices[1] = ((is_outer,), ride["in"], ("is", slot))
                else:
                    choices[1] = ((is_outer,),) + local(c, f"send{slot}")
            pieces.append(choices)
        if pieces:
            after = [got_edge[n - 2]] if n - 2 in got_edge else []
            got_edge[n] = lax.ppermute(packed(pieces, after), "roll", edge_pairs)
        if n == 0:
            ride_first()
        if n == ride_from - 3:
            ride_mix()
        if n == ride_from - 1:
            ride_cores()
        if n == where["out", "ride", 0, 0][0] + 2:
            ride_out()
        for group in list(to_place):
            if swap_round[group[1], group[2][0]] <= n - 2:
                place(group)
                to_place.remove(group)
    if "mixed" not in ride:
        ride_out()
    for group in to_swap:
        swap(group, rounds)
    for group in to_place + to_swap:
        place(group)
    return tuple(outs) + (ride["mixed"],)


def direct_exchange(quants, placement, trains, owners):
    outs = []
    for quant in quants:
        _, experts, blocks, rows, features = quant.shape
        x = lax.all_to_all(quant, "train", split_axis=0, concat_axis=0, tiled=True)
        x = jnp.transpose(x, (1, 2, 3, 0, 4)).reshape(experts, blocks, rows, trains * features)
        picked = jnp.take(x, placement, axis=0)
        got = lax.all_to_all(picked, "roll", split_axis=0, concat_axis=0, tiled=True)
        outs.append(got.reshape(owners * blocks, rows, trains * features))
    return outs


def pre_activation_kernel(experts, top, tok_ref, ids_ref, w_ref, *refs):
    out_ref = refs[-1]
    features = tok_ref.shape[1]
    weights = w_ref[...].reshape(experts * BLOCK, features)
    pre = lax.dot_general(
        tok_ref[...], weights, (((1,), (1,)), ((), ())), preferred_element_type=jnp.float32
    )
    for k in range(top):
        total = jnp.zeros((pre.shape[0], BLOCK), jnp.float32)
        for expert in range(experts):
            part = pre[:, expert * BLOCK : (expert + 1) * BLOCK]
            total = total + jnp.where(ids_ref[:, k : k + 1] == expert, part, 0.0)
        out_ref[:, k * BLOCK : (k + 1) * BLOCK] = total


def pre_activations(tokens, ids, restored, block, out, column, columns, after=()):
    count, features = tokens.shape
    experts, top = restored.shape[0], ids.shape[1]
    tile = min(count, 2 * BLOCK)
    operands = [tokens, ids, restored] + list(after) + ([] if out is None else [out])
    return pl.pallas_call(
        functools.partial(pre_activation_kernel, experts, top),
        grid=(count // tile,),
        in_specs=[
            pl.BlockSpec((tile, features), lambda i: (i, 0)),
            pl.BlockSpec((tile, top), lambda i: (i, 0)),
            pl.BlockSpec((experts, 1, BLOCK, features), lambda i: (0, block, 0, 0)),
        ]
        + [any_spec()] * (len(operands) - 3),
        out_specs=pl.BlockSpec((tile, top * BLOCK), lambda i: (i, column)),
        out_shape=jax.ShapeDtypeStruct((count, columns * top * BLOCK), jnp.float32),
        input_output_aliases={} if out is None else {len(operands) - 1: 0},
        compiler_params=pltpu.CompilerParams(vmem_limit_bytes=VMEM_BYTES),
        cost_estimate=LIGHT,
        name="pre_activations",
    )(*operands)


def mix_rows(experts, top, blocks, pre_ref, ids_ref, weights_ref, down_ref):
    width = top * BLOCK
    count, features = ids_ref.shape[0], down_ref.shape[-1]
    hidden = {}
    for b in range(blocks):
        for k in range(top):
            start = b * width + k * BLOCK
            gate = pre_ref[:, start : start + BLOCK]
            up = pre_ref[:, blocks * width + start : blocks * width + start + BLOCK]
            value = gate / (1.0 + jnp.exp(-gate)) * up
            hidden[b, k] = value.astype(jnp.bfloat16).astype(jnp.float32)
    total = jnp.zeros((count, features), jnp.float32)
    for expert in range(experts):
        weight = jnp.zeros((count, 1), jnp.float32)
        for k in range(top):
            weight = weight + jnp.where(
                ids_ref[:, k : k + 1] == expert, weights_ref[:, k : k + 1], 0.0
            )
        value = jnp.zeros((count, features), jnp.float32)
        for b in range(blocks):
            routed = jnp.zeros((count, BLOCK), jnp.float32)
            for k in range(top):
                routed = routed + jnp.where(ids_ref[:, k : k + 1] == expert, hidden[b, k], 0.0)
            value = value + jnp.dot(
                routed.astype(jnp.bfloat16), down_ref[expert, b], preferred_element_type=jnp.float32
            )
        total = total + weight * value
    return total


def mix_kernel(sizes, pre_ref, ids_ref, weights_ref, down_ref, out_ref):
    out_ref[...] = mix_rows(*sizes, pre_ref, ids_ref, weights_ref, down_ref)


def mix_split_kernel(sizes, core, pre_ref, ids_ref, weights_ref, down_ref, plan_ref, *refs):
    keep_ref, send_ref = refs[-2:]
    total = mix_rows(*sizes, pre_ref, ids_ref, weights_ref, down_ref)
    half = total.shape[0] // CORES
    first = plan_ref[core] == 0
    keep_ref[0] = jnp.where(first, total[:half], total[half:])
    send_ref[...] = jnp.where(first, total[half:], total[:half]).astype(send_ref.dtype)


def mix_specs(pre, ids, down, tile):
    return [
        pl.BlockSpec((tile, pre.shape[1]), lambda i: (i, 0)),
        pl.BlockSpec((tile, ids.shape[1]), lambda i: (i, 0)),
        pl.BlockSpec((tile, ids.shape[1]), lambda i: (i, 0)),
        pl.BlockSpec(down.shape, lambda i: (0, 0, 0, 0)),
    ]


def mix_experts(pre, ids, weights, down, plan=None, places=None, after=()):
    count, top = ids.shape
    experts, blocks, _, features = down.shape
    sizes = (experts, top, blocks)
    tile = min(count, BLOCK)
    params = pltpu.CompilerParams(vmem_limit_bytes=VMEM_BYTES)
    if plan is None:
        return pl.pallas_call(
            functools.partial(mix_kernel, sizes),
            grid=(count // tile,),
            in_specs=mix_specs(pre, ids, down, tile),
            out_specs=pl.BlockSpec((tile, features), lambda i: (i, 0)),
            out_shape=jax.ShapeDtypeStruct((count, features), jnp.float32),
            compiler_params=params,
            cost_estimate=LIGHT,
            name="mix_experts",
        )(pre, ids, weights, down)
    half = tile // CORES
    return pl.pallas_call(
        functools.partial(mix_split_kernel, sizes, places["core"]),
        grid=(count // tile,),
        in_specs=mix_specs(pre, ids, down, tile) + [smem_spec()] + [any_spec()] * len(after),
        out_specs=[
            pl.BlockSpec((1, half, features), lambda i: (i, 0, 0)),
            pl.BlockSpec((half, features), lambda i: (i, 0)),
        ],
        out_shape=[
            jax.ShapeDtypeStruct((count // tile, half, features), jnp.float32),
            jax.ShapeDtypeStruct((count // CORES, features), jnp.bfloat16),
        ],
        compiler_params=params,
        cost_estimate=LIGHT,
        name="mix_experts",
    )(pre, ids, weights, down, plan, *after)


def sum_call(kernel, name, out_shape, plan, arrays, piece, after):
    vmem = pl.BlockSpec(memory_space=pltpu.VMEM)
    operands = [plan] + list(arrays)
    specs = [smem_spec()] + [vmem] * len(arrays)
    if piece is not None:
        array, first, number = piece
        operands += [array] * number
        for n in range(number):
            specs.append(
                pl.BlockSpec((1,) + array.shape[1:], lambda i, n=n: (first + n, 0, 0))
            )
    return pl.pallas_call(
        kernel,
        grid=(1,),
        in_specs=specs + [any_spec()] * len(after),
        out_specs=[vmem] * len(out_shape) if isinstance(out_shape, list) else vmem,
        out_shape=out_shape,
        compiler_params=pltpu.CompilerParams(vmem_limit_bytes=VMEM_BYTES),
        cost_estimate=LIGHT,
        name=name,
    )(*operands, *after)


def sum_cores_kernel(places, plan_ref, keep_ref, got_ref, *refs):
    sums_ref, send_ref = refs[-2:]
    chips, tokens, features = keep_ref.shape
    for chip in range(chips):
        rows = slice(chip * tokens, (chip + 1) * tokens)
        sums_ref[chip] = keep_ref[chip] + got_ref[rows, :].astype(jnp.float32)
    side, chip = plan_ref[places["side"]], plan_ref[places["chip"]]
    for n in range(2):
        send_ref[n * tokens : (n + 1) * tokens, :] = sums_ref[2 * (1 - side) + n].astype(
            send_ref.dtype
        )
    partner = sums_ref[1 + 4 * side - chip].astype(send_ref.dtype)
    for n in range(2, 4):
        send_ref[n * tokens : (n + 1) * tokens, :] = partner


def sum_cores(plan, places, keep, got, after=()):
    _, tokens, features = keep.shape
    out_shape = [
        jax.ShapeDtypeStruct(keep.shape, jnp.float32),
        jax.ShapeDtypeStruct((4 * tokens, features), jnp.bfloat16),
    ]
    kernel = functools.partial(sum_cores_kernel, places)
    return sum_call(kernel, "sum_cores", out_shape, plan, [keep, got], None, after)


def sum_inwards_kernel(places, plan_ref, sums_ref, over_ref, here_ref, *refs):
    inner_ref, send_ref = refs[-2:]
    tokens = inner_ref.shape[0]
    side, chip = plan_ref[places["side"]], plan_ref[places["chip"]]
    for n in range(2):
        rows = slice(n * tokens, (n + 1) * tokens)
        total = sums_ref[2 * (1 - side) + n] + over_ref[0, rows, :].astype(jnp.float32)
        send_ref[rows, :] = total.astype(send_ref.dtype)
    inner_ref[...] = sums_ref[chip] + here_ref[0, :tokens, :].astype(jnp.float32)


def sum_inwards(plan, places, sums, got, first, after=()):
    _, tokens, features = sums.shape
    out_shape = [
        jax.ShapeDtypeStruct((tokens, features), jnp.float32),
        jax.ShapeDtypeStruct((2 * tokens, features), jnp.bfloat16),
    ]
    kernel = functools.partial(sum_inwards_kernel, places)
    return sum_call(kernel, "sum_inwards", out_shape, plan, [sums], (got, first, 2), after)


def sum_across_kernel(places, plan_ref, sums_ref, inner_ref, got_ref, *refs):
    final_ref, send_ref = refs[-2:]
    tokens = inner_ref.shape[0]
    side, chip = plan_ref[places["side"]], plan_ref[places["chip"]]
    place = chip - 2 * side
    low = got_ref[0, :tokens, :].astype(jnp.float32)
    high = got_ref[0, tokens:, :].astype(jnp.float32)
    final_ref[...] = inner_ref[...] + jnp.where(place == 0, low, high)
    total = sums_ref[1 + 4 * side - chip] + jnp.where(place == 0, high, low)
    for n in range(2):
        send_ref[n * tokens : (n + 1) * tokens, :] = total.astype(send_ref.dtype)


def sum_across(plan, places, sums, inner, got, first, after=()):
    _, tokens, features = sums.shape
    out_shape = [
        jax.ShapeDtypeStruct((tokens, features), jnp.float32),
        jax.ShapeDtypeStruct((2 * tokens, features), jnp.bfloat16),
    ]
    kernel = functools.partial(sum_across_kernel, places)
    return sum_call(kernel, "sum_across", out_shape, plan, [sums, inner], (got, first, 1), after)


def sum_outwards_kernel(places, plan_ref, sums_ref, final_ref, got_ref, *refs):
    out_ref = refs[-1]
    tokens = final_ref.shape[0]
    outer = sums_ref[plan_ref[places["chip"]]] + got_ref[0, :tokens, :].astype(jnp.float32)
    out_ref[...] = jnp.where(plan_ref[places["inner"]] == 1, final_ref[...], outer).astype(
        out_ref.dtype
    )


def sum_outwards(plan, places, sums, final, got, first, after=()):
    out_shape = jax.ShapeDtypeStruct(final.shape, jnp.bfloat16)
    kernel = functools.partial(sum_outwards_kernel, places)
    return sum_call(kernel, "sum_outwards", out_shape, plan, [sums, final], (got, first, 1), after)


def gather_tokens(tokens, expert_ids, gate_weights, features):
    mine = lax.dynamic_slice_in_dim(tokens, lax.axis_index("train") * features, features, axis=1)
    top = expert_ids.shape[1]
    high = lax.reduce_precision(gate_weights, 8, 7)
    middle = lax.reduce_precision(gate_weights - high, 8, 7)
    low = gate_weights - high - middle
    beside = jnp.concatenate((expert_ids.astype(jnp.float32), high, middle, low), axis=1)
    beside = jnp.pad(beside, ((0, 0), (0, BLOCK - 4 * top))).astype(jnp.bfloat16)
    every = lax.all_gather(jnp.concatenate((mine, beside), axis=1), "roll", axis=0, tiled=True)
    side = every[:, features : features + 4 * top].astype(jnp.float32)
    ids = side[:, :top].astype(jnp.int32)
    weights = side[:, top : 2 * top] + side[:, 2 * top : 3 * top] + side[:, 3 * top :]
    return every[:, :features], ids, weights


def per_device(master_gate, master_up, master_down, tokens, expert_ids, gate_weights, placement):
    trains = lax.axis_size("train")
    owners = lax.axis_size("roll")
    experts, hidden_rows, features = master_gate.shape
    blocks = hidden_rows // BLOCK
    if owners // CORES == 4 and CORES * tokens.shape[0] == BLOCK:
        quant, gate = quantize(master_gate, 0, 1, trains, experts)
        x_first = lax.all_to_all(quant, "train", split_axis=0, concat_axis=0, tiled=True)
        plan, places = make_plan(placement, experts, owners, (quant,))
        quants, dequant, after = [], [gate], plan
        if blocks > 1:
            after, gate = quantize(master_gate, 1, blocks - 1, trains, experts, 0, None, (plan,))
            quants.append(after)
            dequant.append(gate)
        rest, up = quantize(master_up, 0, blocks, trains, 2 * experts, 0, None, (after,))
        rest, down = quantize(master_down, 0, blocks, trains, 2 * experts, experts, rest)
        quants.append(rest)
        dequant += [up, down]
        routed = gather_tokens(tokens, expert_ids, gate_weights, features)
        most = min(experts, owners // 2)
        shapes = (experts, blocks, trains, owners)

        def branch(cap, x_first, quants, dequant, plan, routed):
            return line_exchange(x_first, quants, dequant, plan, places, routed, shapes, cap)

        outs = lax.cond(
            plan[places["most"]] <= most - 1,
            functools.partial(branch, most - 1),
            functools.partial(branch, most),
            x_first,
            quants,
            dequant,
            plan,
            routed,
        )
    else:
        masters = (master_gate, master_up, master_down)
        quants, dequant = zip(*[quantize(w, 0, blocks, trains, experts) for w in masters])
        every, ids, weights = gather_tokens(tokens, expert_ids, gate_weights, features)
        outs = direct_exchange(quants, placement, trains, owners)
        pre = None
        for n in range(2 * blocks):
            restored = dequant[n // blocks]
            pre = pre_activations(every, ids, restored, n % blocks, pre, n, 2 * blocks)
        mixed = mix_experts(lax.psum(pre, "train"), ids, weights, dequant[2])
        mixed = lax.psum_scatter(mixed, "roll", scatter_dimension=0, tiled=True)
        outs = tuple(outs) + (mixed.astype(jnp.bfloat16),)
    return tuple(out[None] for out in outs[:3]) + (outs[3],)


def solution(mesh):
    in_specs = (
        P(None, "roll", "train"),
        P(None, "roll", "train"),
        P(None, "roll", "train"),
        P("roll", None),
        P("roll", None),
        P("roll", None),
        P(),
    )
    out_specs = (
        P("roll", None, "train", None),
        P("roll", None, "train", None),
        P("roll", None, "train", None),
        P("roll", "train"),
    )
    return jax.shard_map(
        per_device, mesh=mesh, in_specs=in_specs, out_specs=out_specs, check_vma=False
    )
```

profile of v0, /device:TPU:19, one launch (start us, length us, event | category | flops | bytes accessed | tf_op | source)
XLA Modules:
  0.0 543.9 jit_solution(18291827449042835643)
XLA Ops:
  25.1 9.9 %quantize.6 = (bf16[4,8,2,32,1792]{4,3,2,1,0:T(8,128)(2,1)}, bf16[4,2,128,1792]{3,2,1,0:T(8,128)(2,1)}) custom-call(f32[4,256,1792]{2,1,0:T(8,128)} %x_ref.6, bf16[4,4,1,32,1792]{4,3,2,1,0:T(8,128)(2,1)S(1)} %get-tuple-element.145.refs_0_), custom_call_target="tpu_custom_call" | custom-call | flops 1 | bytes 1 | tf_op jit(solution)/shard_map/quantize/pallas_call | solution.py:42
  35.0 9.3 %quantize.7 = (bf16[4,8,2,32,1792]{4,3,2,1,0:T(8,128)(2,1)}, bf16[4,2,128,1792]{3,2,1,0:T(8,128)(2,1)}) custom-call(f32[4,256,1792]{2,1,0:T(8,128)} %x_ref.7, bf16[4,8,2,32,1792]{4,3,2,1,0:T(8,128)(2,1)} %get-tuple-element.149.refs_0_), custom_call_target="tpu_custom_call", output_to_operand_aliasing={{0}: (1, {})} | custom-call | flops 1 | bytes 1 | tf_op jit(solution)/shard_map/quantize/pallas_call | solution.py:42
  49.7 486.2 %conditional.1 = (bf16[16,32,7168]{2,1,0:T(8,128)(2,1)}, bf16[16,32,7168]{2,1,0:T(8,128)(2,1)}, bf16[16,32,7168]{2,1,0:T(8,128)(2,1)}, bf16[64,1792]{1,0:T(8,128)(2,1)}) conditional(s32[]{:T(128)} %bitcast.17, (bf16[4,4,1,32,1792]{4,3,2,1,0:T(8,128)(2,1)}, s32[29]{0:T(128)S(1)}, bf16[4,4,1,32,1792]{4,3,2,1,0:T(8,128)(2,1)}, ...), branch_computations={%region_0.2_spmd, %region_2.4_spmd} | conditional | flops 524347 | bytes 549063424 | solution.py:826
  51.3 23.9 %all_to_all.22.refs_0_.refs_2_ = bf16[4,4,1,32,1792]{4,3,2,1,0:T(8,128)(2,1)S(1)} all-to-all(bf16[4,4,1,32,1792]{4,3,2,1,0:T(8,128)(2,1)} %get-tuple-element.87), channel_id=1, replica_groups=mesh['train'=4,'roll'=8] {'train'}, dimensions={0} | all-to-all | bytes 3670016 | tf_op jit(solution)/shard_map/cond/branch_1_fun/all_to_all | solution.py:341
  75.2 6.0 %all-to-all-start.3 = ((bf16[4,8,2,32,1792]{4,3,2,1,0:T(8,128)(2,1)}), bf16[4,8,2,32,1792]{4,3,2,1,0:T(8,128)(2,1)}, u32[]{:S(2)}, u32[]{:S(2)}) async-start(bf16[4,8,2,32,1792]{4,3,2,1,0:T(8,128)(2,1)} %get-tuple-element.94), calls=%async_computation.3 | async-start | bytes 14680064 | tf_op jit(solution)/shard_map/cond/branch_1_fun/all_to_all | solution.py:341
  108.9 7.1 %collective-permute-done.42.refs_0_.refs_4_.refs_1_ = bf16[3,4,1,32,1792]{4,3,2,1,0:T(8,128)(2,1)S(1)} collective-permute-done((bf16[3,4,1,32,1792]{4,3,2,1,0:T(8,128)(2,1)}, bf16[3,4,1,32,1792]{4,3,2,1,0:T(8,128)(2,1)S(1)}, u32[]{:S(2)}, u32[]{:S(2)}) %collective-permute-start.42) | collective-permute-done | bytes 1376288 | tf_op jit(solution)/shard_map/cond/branch_1_fun/ppermute | solution.py:518
  122.3 7.4 %collective-permute-start.46 = (bf16[2,4,1,32,1792]{4,3,2,1,0:T(8,128)(2,1)}, bf16[2,4,1,32,1792]{4,3,2,1,0:T(8,128)(2,1)S(1)}, u32[]{:S(2)}, u32[]{:S(2)}) collective-permute-start(bf16[2,4,1,32,1792]{4,3,2,1,0:T(8,128)(2,1)} %pack.119.refs_1_), channel_id=1, source_target_pairs={{0,2},{2,0},{4,6},{6,4},{1,3},{3,1},{5,7},{7,5},{8,10},{10,8},{12,... | collective-permute-start | bytes 2752520 | tf_op jit(solution)/shard_map/cond/branch_1_fun/ppermute | solution.py:518
  129.7 15.7 %collective-permute-done.40.refs_0_.refs_3_.refs_1_ = bf16[3,4,1,32,1792]{4,3,2,1,0:T(8,128)(2,1)} collective-permute-done((bf16[3,4,1,32,1792]{4,3,2,1,0:T(8,128)(2,1)}, bf16[3,4,1,32,1792]{4,3,2,1,0:T(8,128)(2,1)}, u32[]{:S(2)}, u32[]{:S(2)}) %collective-permute-start.40) | collective-permute-done | bytes 1376288 | tf_op jit(solution)/shard_map/cond/branch_1_fun/ppermute | solution.py:518
  151.2 13.9 %collective-permute-done.46.refs_2_.refs_3_.refs_1_ = bf16[2,4,1,32,1792]{4,3,2,1,0:T(8,128)(2,1)S(1)} collective-permute-done((bf16[2,4,1,32,1792]{4,3,2,1,0:T(8,128)(2,1)}, bf16[2,4,1,32,1792]{4,3,2,1,0:T(8,128)(2,1)S(1)}, u32[]{:S(2)}, u32[]{:S(2)}) %collective-permute-start.46) | collective-permute-done | bytes 917536 | tf_op jit(solution)/shard_map/cond/branch_1_fun/ppermute | solution.py:518
  170.5 5.4 %collective-permute-done.45.refs_2_.refs_0_ = bf16[3,4,1,32,1792]{4,3,2,1,0:T(8,128)(2,1)} collective-permute-done((bf16[3,4,1,32,1792]{4,3,2,1,0:T(8,128)(2,1)}, bf16[3,4,1,32,1792]{4,3,2,1,0:T(8,128)(2,1)}, u32[]{:S(2)}, u32[]{:S(2)}) %collective-permute-start.45) | collective-permute-done | bytes 1376288 | tf_op jit(solution)/shard_map/cond/branch_1_fun/ppermute | solution.py:494
  181.6 9.4 %collective-permute-start.43 = (bf16[2,4,1,32,1792]{4,3,2,1,0:T(8,128)(2,1)S(1)}, bf16[2,4,1,32,1792]{4,3,2,1,0:T(8,128)(2,1)S(1)}, u32[]{:S(2)}, u32[]{:S(2)}) collective-permute-start(bf16[2,4,1,32,1792]{4,3,2,1,0:T(8,128)(2,1)S(1)} %copy-done.77), channel_id=1, source_target_pairs={{0,2},{2,0},{4,6},{6,4},{1,3},{3,1},{5,7},{7,5},{8,10},{10,8},{12,... | collective-permute-start | bytes 2752520 | tf_op jit(solution)/shard_map/cond/branch_1_fun/ppermute | solution.py:518
  191.2 14.3 %collective-permute-done.44.refs_2_.refs_0_ = bf16[3,4,1,32,1792]{4,3,2,1,0:T(8,128)(2,1)} collective-permute-done((bf16[3,4,1,32,1792]{4,3,2,1,0:T(8,128)(2,1)}, bf16[3,4,1,32,1792]{4,3,2,1,0:T(8,128)(2,1)}, u32[]{:S(2)}, u32[]{:S(2)}) %collective-permute-start.44) | collective-permute-done | bytes 1376288 | tf_op jit(solution)/shard_map/cond/branch_1_fun/ppermute | solution.py:494
  205.5 8.0 %collective-permute-start.49 = (bf16[2,4,1,32,1792]{4,3,2,1,0:T(8,128)(2,1)}, bf16[2,4,1,32,1792]{4,3,2,1,0:T(8,128)(2,1)}, u32[]{:S(2)}, u32[]{:S(2)}) collective-permute-start(bf16[2,4,1,32,1792]{4,3,2,1,0:T(8,128)(2,1)} %pack.122.refs_3_), channel_id=1, source_target_pairs={{0,1},{2,3},{4,5},{6,7},{1,0},{3,2},{5,4},{7,6},{8,9},{10,11},{12,... | collective-permute-start | bytes 2752520 | tf_op jit(solution)/shard_map/cond/branch_1_fun/ppermute | solution.py:411
  216.2 8.5 %collective-permute-done.43.refs_3_.refs_1_ = bf16[2,4,1,32,1792]{4,3,2,1,0:T(8,128)(2,1)S(1)} collective-permute-done((bf16[2,4,1,32,1792]{4,3,2,1,0:T(8,128)(2,1)S(1)}, bf16[2,4,1,32,1792]{4,3,2,1,0:T(8,128)(2,1)S(1)}, u32[]{:S(2)}, u32[]{:S(2)}) %collective-permute-start.43) | collective-permute-done | bytes 917536 | tf_op jit(solution)/shard_map/cond/branch_1_fun/ppermute | solution.py:518
  231.2 7.9 %mix_experts.3 = (f32[4,64,1792]{2,1,0:T(8,128)S(1)}, bf16[256,1792]{1,0:T(8,128)(2,1)}) custom-call(f32[512,1024]{1,0:T(8,128)S(1)} %copy-done.78, s32[512,2]{1,0:T(8,128)S(1)} %copy-done.98, f32[512,2]{1,0:T(8,128)} %copy-done.104, bf16[4,2,128,1792]{3,2,1,0:T(8,128)(2,1)} %get-tuple-element.96.down_ref, s32[29]{0:T(128)S(1)} %get-tuple-element.86.plan_ref, ...), custom_call_target="tpu_custom_call" | custom-call | flops 1 | bytes 1 | tf_op jit(solution)/shard_map/cond/branch_1_fun/mix_experts/pallas_call | solution.py:660
  250.5 11.8 %collective-permute-start.60 = (bf16[3,4,1,32,1792]{4,3,2,1,0:T(8,128)(2,1)}, bf16[3,4,1,32,1792]{4,3,2,1,0:T(8,128)(2,1)S(1)}, u32[]{:S(2)}, u32[]{:S(2)}) collective-permute-start(bf16[3,4,1,32,1792]{4,3,2,1,0:T(8,128)(2,1)} %pack.131.refs_4_), channel_id=1, source_target_pairs={{0,2},{2,0},{4,6},{6,4},{1,3},{3,1},{5,7},{7,5},{8,10},{10,8},{12,... | collective-permute-start | bytes 4128776 | tf_op jit(solution)/shard_map/cond/branch_1_fun/ppermute | solution.py:518
  263.5 8.1 %collective-permute-start.56 = (bf16[1,4,1,32,1792]{4,3,2,1,0:T(8,128)(2,1)}, bf16[1,4,1,32,1792]{4,3,2,1,0:T(8,128)(2,1)}, u32[]{:S(2)}, u32[]{:S(2)}) collective-permute-start(bf16[1,4,1,32,1792]{4,3,2,1,0:T(8,128)(2,1)} %pack.129.refs_1_), channel_id=1, source_target_pairs={{0,1},{2,3},{4,5},{6,7},{1,0},{3,2},{5,4},{7,6},{8,9},{10,11},{12,... | collective-permute-start | bytes 1376264 | tf_op jit(solution)/shard_map/cond/branch_1_fun/ppermute | solution.py:411
  311.1 11.0 %collective-permute-done.55.refs_0_.refs_3_.refs_1_.refs_4_ = bf16[3,4,1,32,1792]{4,3,2,1,0:T(8,128)(2,1)S(1)} collective-permute-done((bf16[3,4,1,32,1792]{4,3,2,1,0:T(8,128)(2,1)}, bf16[3,4,1,32,1792]{4,3,2,1,0:T(8,128)(2,1)S(1)}, u32[]{:S(2)}, u32[]{:S(2)}) %collective-permute-start.55) | collective-permute-done | bytes 1376288 | tf_op jit(solution)/shard_map/cond/branch_1_fun/ppermute | solution.py:518
  333.7 17.8 %collective-permute-done.63.refs_2_.refs_3_.refs_4_ = bf16[3,4,1,32,1792]{4,3,2,1,0:T(8,128)(2,1)S(1)} collective-permute-done((bf16[3,4,1,32,1792]{4,3,2,1,0:T(8,128)(2,1)S(1)}, bf16[3,4,1,32,1792]{4,3,2,1,0:T(8,128)(2,1)S(1)}, u32[]{:S(2)}, u32[]{:S(2)}) %collective-permute-start.63) | collective-permute-done | bytes 1376288 | tf_op jit(solution)/shard_map/cond/branch_1_fun/ppermute | solution.py:518
  367.3 19.2 %collective-permute-done.61.refs_2_.refs_3_.refs_4_.refs_1_ = bf16[3,4,1,32,1792]{4,3,2,1,0:T(8,128)(2,1)S(1)} collective-permute-done((bf16[3,4,1,32,1792]{4,3,2,1,0:T(8,128)(2,1)}, bf16[3,4,1,32,1792]{4,3,2,1,0:T(8,128)(2,1)S(1)}, u32[]{:S(2)}, u32[]{:S(2)}) %collective-permute-start.61) | collective-permute-done | bytes 1376288 | tf_op jit(solution)/shard_map/cond/branch_1_fun/ppermute | solution.py:518
  395.4 37.7 %collective-permute-done.66.refs_2_.refs_0_.refs_6_ = bf16[3,4,1,32,1792]{4,3,2,1,0:T(8,128)(2,1)} collective-permute-done((bf16[3,4,1,32,1792]{4,3,2,1,0:T(8,128)(2,1)}, bf16[3,4,1,32,1792]{4,3,2,1,0:T(8,128)(2,1)}, u32[]{:S(2)}, u32[]{:S(2)}) %collective-permute-start.66) | collective-permute-done | bytes 1376288 | tf_op jit(solution)/shard_map/cond/branch_1_fun/ppermute | solution.py:494
  449.1 19.6 %collective-permute-done.72.refs_3_.refs_2_ = bf16[3,4,1,32,1792]{4,3,2,1,0:T(8,128)(2,1)} collective-permute-done((bf16[3,4,1,32,1792]{4,3,2,1,0:T(8,128)(2,1)}, bf16[3,4,1,32,1792]{4,3,2,1,0:T(8,128)(2,1)}, u32[]{:S(2)}, u32[]{:S(2)}) %collective-permute-start.72) | collective-permute-done | bytes 1376288 | tf_op jit(solution)/shard_map/cond/branch_1_fun/ppermute | solution.py:518
  492.1 6.1 %collective-permute-done.74.refs_1_ = bf16[3,4,1,32,1792]{4,3,2,1,0:T(8,128)(2,1)} collective-permute-done((bf16[3,4,1,32,1792]{4,3,2,1,0:T(8,128)(2,1)}, bf16[3,4,1,32,1792]{4,3,2,1,0:T(8,128)(2,1)}, u32[]{:S(2)}, u32[]{:S(2)}) %collective-permute-start.74) | collective-permute-done | bytes 1376288 | tf_op jit(solution)/shard_map/cond/branch_1_fun/ppermute | solution.py:518
  501.5 16.3 %collective-permute-done.73.refs_5_ = bf16[2,4,1,32,1792]{4,3,2,1,0:T(8,128)(2,1)S(1)} collective-permute-done((bf16[2,4,1,32,1792]{4,3,2,1,0:T(8,128)(2,1)}, bf16[2,4,1,32,1792]{4,3,2,1,0:T(8,128)(2,1)S(1)}, u32[]{:S(2)}, u32[]{:S(2)}) %collective-permute-start.73) | collective-permute-done | bytes 917536 | tf_op jit(solution)/shard_map/cond/branch_1_fun/ppermute | solution.py:518
  (257 shorter events, 233.3 us)
Async XLA Ops:
  7.2 38.4 %all-gather.2.cloned.1.call-start = ((), (), s32[]{:S(2)}) async-start(), calls=%async_computation.7 | async-start | bytes 2211840 | tf_op jit(solution)/shard_map/all_gather | solution.py:794
  75.2 100.8 %all-to-all-start.3 = ((bf16[4,8,2,32,1792]{4,3,2,1,0:T(8,128)(2,1)}), bf16[4,8,2,32,1792]{4,3,2,1,0:T(8,128)(2,1)}, u32[]{:S(2)}, u32[]{:S(2)}) async-start(bf16[4,8,2,32,1792]{4,3,2,1,0:T(8,128)(2,1)} %get-tuple-element.94), calls=%async_computation.3 | async-start | bytes 14680064 | tf_op jit(solution)/shard_map/cond/branch_1_fun/all_to_all | solution.py:341
  103.2 126.3 %all-reduce.6.cloned.1.call-start = ((), (), s32[]{:S(2)}) async-start(), calls=%async_computation.6 | async-start | bytes 4194304 | tf_op jit(solution)/shard_map/cond/branch_1_fun/psum | solution.py:436
  106.2 39.3 %collective-permute-start.40 = (bf16[3,4,1,32,1792]{4,3,2,1,0:T(8,128)(2,1)}, bf16[3,4,1,32,1792]{4,3,2,1,0:T(8,128)(2,1)}, u32[]{:S(2)}, u32[]{:S(2)}) collective-permute-start(bf16[3,4,1,32,1792]{4,3,2,1,0:T(8,128)(2,1)} %pack.117.refs_1_), channel_id=1, source_target_pairs={{0,2},{2,0},{4,6},{6,4},{1,3},{3,1},{5,7},{7,5},{8,10},{10,8},{12,... | collective-permute-start | bytes 4128776 | tf_op jit(solution)/shard_map/cond/branch_1_fun/ppermute | solution.py:518
  108.8 37.7 %collective-permute-start.39 = (bf16[3,4,1,32,1792]{4,3,2,1,0:T(8,128)(2,1)}, bf16[3,4,1,32,1792]{4,3,2,1,0:T(8,128)(2,1)S(1)}, u32[]{:S(2)}, u32[]{:S(2)}) collective-permute-start(bf16[3,4,1,32,1792]{4,3,2,1,0:T(8,128)(2,1)} %pack.116.refs_2_), channel_id=1, source_target_pairs={{2,4},{4,2},{0,1},{6,7},{3,5},{5,3},{1,0},{7,6},{10,12},{12,10},{8... | collective-permute-start | bytes 4128776 | tf_op jit(solution)/shard_map/cond/branch_1_fun/ppermute | solution.py:494
  119.5 56.5 %collective-permute-start.45 = (bf16[3,4,1,32,1792]{4,3,2,1,0:T(8,128)(2,1)}, bf16[3,4,1,32,1792]{4,3,2,1,0:T(8,128)(2,1)}, u32[]{:S(2)}, u32[]{:S(2)}) collective-permute-start(bf16[3,4,1,32,1792]{4,3,2,1,0:T(8,128)(2,1)} %pack.118.refs_3_), channel_id=1, source_target_pairs={{2,4},{4,2},{0,1},{6,7},{3,5},{5,3},{1,0},{7,6},{10,12},{12,10},{8... | collective-permute-start | bytes 4128776 | tf_op jit(solution)/shard_map/cond/branch_1_fun/ppermute | solution.py:494
  122.3 42.8 %collective-permute-start.46 = (bf16[2,4,1,32,1792]{4,3,2,1,0:T(8,128)(2,1)}, bf16[2,4,1,32,1792]{4,3,2,1,0:T(8,128)(2,1)S(1)}, u32[]{:S(2)}, u32[]{:S(2)}) collective-permute-start(bf16[2,4,1,32,1792]{4,3,2,1,0:T(8,128)(2,1)} %pack.119.refs_1_), channel_id=1, source_target_pairs={{0,2},{2,0},{4,6},{6,4},{1,3},{3,1},{5,7},{7,5},{8,10},{10,8},{12,... | collective-permute-start | bytes 2752520 | tf_op jit(solution)/shard_map/cond/branch_1_fun/ppermute | solution.py:518
  149.2 56.3 %collective-permute-start.44 = (bf16[3,4,1,32,1792]{4,3,2,1,0:T(8,128)(2,1)}, bf16[3,4,1,32,1792]{4,3,2,1,0:T(8,128)(2,1)}, u32[]{:S(2)}, u32[]{:S(2)}) collective-permute-start(bf16[3,4,1,32,1792]{4,3,2,1,0:T(8,128)(2,1)} %pack.120.refs_2_), channel_id=1, source_target_pairs={{2,4},{4,2},{0,1},{6,7},{3,5},{5,3},{1,0},{7,6},{10,12},{12,10},{8... | collective-permute-start | bytes 4128776 | tf_op jit(solution)/shard_map/cond/branch_1_fun/ppermute | solution.py:494
  181.1 46.6 %collective-permute-start.51 = (bf16[3,4,1,32,1792]{4,3,2,1,0:T(8,128)(2,1)S(1)}, bf16[3,4,1,32,1792]{4,3,2,1,0:T(8,128)(2,1)S(1)}, u32[]{:S(2)}, u32[]{:S(2)}) collective-permute-start(bf16[3,4,1,32,1792]{4,3,2,1,0:T(8,128)(2,1)S(1)} %pack.125.refs_1_), channel_id=1, source_target_pairs={{0,2},{2,0},{4,6},{6,4},{1,3},{3,1},{5,7},{7,5},{8,10},{10,8},{12,... | collective-permute-start | bytes 4128776 | tf_op jit(solution)/shard_map/cond/branch_1_fun/ppermute | solution.py:518
  181.2 64.1 %collective-permute-start.50 = (bf16[3,4,1,32,1792]{4,3,2,1,0:T(8,128)(2,1)}, bf16[3,4,1,32,1792]{4,3,2,1,0:T(8,128)(2,1)}, u32[]{:S(2)}, u32[]{:S(2)}) collective-permute-start(bf16[3,4,1,32,1792]{4,3,2,1,0:T(8,128)(2,1)} %pack.124.refs_2_), channel_id=1, source_target_pairs={{2,4},{4,2},{0,1},{6,7},{3,5},{5,3},{1,0},{7,6},{10,12},{12,10},{8... | collective-permute-start | bytes 4128776 | tf_op jit(solution)/shard_map/cond/branch_1_fun/ppermute | solution.py:494
  181.6 43.1 %collective-permute-start.43 = (bf16[2,4,1,32,1792]{4,3,2,1,0:T(8,128)(2,1)S(1)}, bf16[2,4,1,32,1792]{4,3,2,1,0:T(8,128)(2,1)S(1)}, u32[]{:S(2)}, u32[]{:S(2)}) collective-permute-start(bf16[2,4,1,32,1792]{4,3,2,1,0:T(8,128)(2,1)S(1)} %copy-done.77), channel_id=1, source_target_pairs={{0,2},{2,0},{4,6},{6,4},{1,3},{3,1},{5,7},{7,5},{8,10},{10,8},{12,... | collective-permute-start | bytes 2752520 | tf_op jit(solution)/shard_map/cond/branch_1_fun/ppermute | solution.py:518
  190.9 71.3 %collective-permute-start.48 = (bf16[2,4,1,32,1792]{4,3,2,1,0:T(8,128)(2,1)}, bf16[2,4,1,32,1792]{4,3,2,1,0:T(8,128)(2,1)}, u32[]{:S(2)}, u32[]{:S(2)}) collective-permute-start(bf16[2,4,1,32,1792]{4,3,2,1,0:T(8,128)(2,1)} %pack.123.refs_1_), channel_id=1, source_target_pairs={{0,1},{2,3},{4,5},{6,7},{1,0},{3,2},{5,4},{7,6},{8,9},{10,11},{12,... | collective-permute-start | bytes 2752520 | tf_op jit(solution)/shard_map/cond/branch_1_fun/ppermute | solution.py:411
  205.5 56.8 %collective-permute-start.49 = (bf16[2,4,1,32,1792]{4,3,2,1,0:T(8,128)(2,1)}, bf16[2,4,1,32,1792]{4,3,2,1,0:T(8,128)(2,1)}, u32[]{:S(2)}, u32[]{:S(2)}) collective-permute-start(bf16[2,4,1,32,1792]{4,3,2,1,0:T(8,128)(2,1)} %pack.122.refs_3_), channel_id=1, source_target_pairs={{0,1},{2,3},{4,5},{6,7},{1,0},{3,2},{5,4},{7,6},{8,9},{10,11},{12,... | collective-permute-start | bytes 2752520 | tf_op jit(solution)/shard_map/cond/branch_1_fun/ppermute | solution.py:411
  250.5 42.0 %collective-permute-start.60 = (bf16[3,4,1,32,1792]{4,3,2,1,0:T(8,128)(2,1)}, bf16[3,4,1,32,1792]{4,3,2,1,0:T(8,128)(2,1)S(1)}, u32[]{:S(2)}, u32[]{:S(2)}) collective-permute-start(bf16[3,4,1,32,1792]{4,3,2,1,0:T(8,128)(2,1)} %pack.131.refs_4_), channel_id=1, source_target_pairs={{0,2},{2,0},{4,6},{6,4},{1,3},{3,1},{5,7},{7,5},{8,10},{10,8},{12,... | collective-permute-start | bytes 4128776 | tf_op jit(solution)/shard_map/cond/branch_1_fun/ppermute | solution.py:518
  263.1 37.7 %collective-permute-start.57 = (bf16[2,4,1,32,1792]{4,3,2,1,0:T(8,128)(2,1)}, bf16[2,4,1,32,1792]{4,3,2,1,0:T(8,128)(2,1)}, u32[]{:S(2)}, u32[]{:S(2)}) collective-permute-start(bf16[2,4,1,32,1792]{4,3,2,1,0:T(8,128)(2,1)} %pack.128.refs_1_), channel_id=1, source_target_pairs={{0,1},{2,3},{4,5},{6,7},{1,0},{3,2},{5,4},{7,6},{8,9},{10,11},{12,... | collective-permute-start | bytes 2752520 | tf_op jit(solution)/shard_map/cond/branch_1_fun/ppermute | solution.py:411
  263.5 37.0 %collective-permute-start.56 = (bf16[1,4,1,32,1792]{4,3,2,1,0:T(8,128)(2,1)}, bf16[1,4,1,32,1792]{4,3,2,1,0:T(8,128)(2,1)}, u32[]{:S(2)}, u32[]{:S(2)}) collective-permute-start(bf16[1,4,1,32,1792]{4,3,2,1,0:T(8,128)(2,1)} %pack.129.refs_1_), channel_id=1, source_target_pairs={{0,1},{2,3},{4,5},{6,7},{1,0},{3,2},{5,4},{7,6},{8,9},{10,11},{12,... | collective-permute-start | bytes 1376264 | tf_op jit(solution)/shard_map/cond/branch_1_fun/ppermute | solution.py:411
  299.7 51.9 %collective-permute-start.63 = (bf16[3,4,1,32,1792]{4,3,2,1,0:T(8,128)(2,1)S(1)}, bf16[3,4,1,32,1792]{4,3,2,1,0:T(8,128)(2,1)S(1)}, u32[]{:S(2)}, u32[]{:S(2)}) collective-permute-start(bf16[3,4,1,32,1792]{4,3,2,1,0:T(8,128)(2,1)S(1)} %pack.136.refs_5_), channel_id=1, source_target_pairs={{0,2},{2,0},{4,6},{6,4},{1,3},{3,1},{5,7},{7,5},{8,10},{10,8},{12,... | collective-permute-start | bytes 4128776 | tf_op jit(solution)/shard_map/cond/branch_1_fun/ppermute | solution.py:518
  300.5 59.5 %collective-permute-start.62 = (bf16[3,4,1,32,1792]{4,3,2,1,0:T(8,128)(2,1)}, bf16[3,4,1,32,1792]{4,3,2,1,0:T(8,128)(2,1)}, u32[]{:S(2)}, u32[]{:S(2)}) collective-permute-start(bf16[3,4,1,32,1792]{4,3,2,1,0:T(8,128)(2,1)} %pack.135.refs_3_), channel_id=1, source_target_pairs={{2,4},{4,2},{0,1},{6,7},{3,5},{5,3},{1,0},{7,6},{10,12},{12,10},{8... | collective-permute-start | bytes 4128776 | tf_op jit(solution)/shard_map/cond/branch_1_fun/ppermute | solution.py:494
  362.8 78.2 %collective-permute-start.70 = (bf16[4,4,1,32,1792]{4,3,2,1,0:T(8,128)(2,1)}, bf16[4,4,1,32,1792]{4,3,2,1,0:T(8,128)(2,1)}, u32[]{:S(2)}, u32[]{:S(2)}) collective-permute-start(bf16[4,4,1,32,1792]{4,3,2,1,0:T(8,128)(2,1)} %pack.141.refs_3_), channel_id=1, source_target_pairs={{2,4},{4,2},{0,1},{6,7},{3,5},{5,3},{1,0},{7,6},{10,12},{12,10},{8... | collective-permute-start | bytes 5505032 | tf_op jit(solution)/shard_map/cond/branch_1_fun/ppermute | solution.py:494
  362.9 70.2 %collective-permute-start.66 = (bf16[3,4,1,32,1792]{4,3,2,1,0:T(8,128)(2,1)}, bf16[3,4,1,32,1792]{4,3,2,1,0:T(8,128)(2,1)}, u32[]{:S(2)}, u32[]{:S(2)}) collective-permute-start(bf16[3,4,1,32,1792]{4,3,2,1,0:T(8,128)(2,1)} %pack.137.refs_2_), channel_id=1, source_target_pairs={{2,4},{4,2},{0,1},{6,7},{3,5},{5,3},{1,0},{7,6},{10,12},{12,10},{8... | collective-permute-start | bytes 4128776 | tf_op jit(solution)/shard_map/cond/branch_1_fun/ppermute | solution.py:494
  367.0 76.7 %collective-permute-start.71 = (bf16[3,4,1,32,1792]{4,3,2,1,0:T(8,128)(2,1)}, bf16[3,4,1,32,1792]{4,3,2,1,0:T(8,128)(2,1)S(1)}, u32[]{:S(2)}, u32[]{:S(2)}) collective-permute-start(bf16[3,4,1,32,1792]{4,3,2,1,0:T(8,128)(2,1)} %pack.142.refs_5_), channel_id=1, source_target_pairs={{0,2},{2,0},{4,6},{6,4},{1,3},{3,1},{5,7},{7,5},{8,10},{10,8},{12,... | collective-permute-start | bytes 4128776 | tf_op jit(solution)/shard_map/cond/branch_1_fun/ppermute | solution.py:518
  438.7 41.4 %collective-permute-start.67 = (bf16[3,4,1,32,1792]{4,3,2,1,0:T(8,128)(2,1)}, bf16[3,4,1,32,1792]{4,3,2,1,0:T(8,128)(2,1)}, u32[]{:S(2)}, u32[]{:S(2)}) collective-permute-start(bf16[3,4,1,32,1792]{4,3,2,1,0:T(8,128)(2,1)} %pack.146.refs_3_), channel_id=1, source_target_pairs={{2,4},{4,2},{0,1},{6,7},{3,5},{5,3},{1,0},{7,6},{10,12},{12,10},{8... | collective-permute-start | bytes 4128776 | tf_op jit(solution)/shard_map/cond/branch_1_fun/ppermute | solution.py:494
  446.5 51.7 %collective-permute-start.74 = (bf16[3,4,1,32,1792]{4,3,2,1,0:T(8,128)(2,1)}, bf16[3,4,1,32,1792]{4,3,2,1,0:T(8,128)(2,1)}, u32[]{:S(2)}, u32[]{:S(2)}) collective-permute-start(bf16[3,4,1,32,1792]{4,3,2,1,0:T(8,128)(2,1)} %pack.148.refs_5_), channel_id=1, source_target_pairs={{0,2},{2,0},{4,6},{6,4},{1,3},{3,1},{5,7},{7,5},{8,10},{10,8},{12,... | collective-permute-start | bytes 4128776 | tf_op jit(solution)/shard_map/cond/branch_1_fun/ppermute | solution.py:518
  448.9 36.9 %collective-permute-start.64 = (bf16[2,4,1,32,1792]{4,3,2,1,0:T(8,128)(2,1)}, bf16[2,4,1,32,1792]{4,3,2,1,0:T(8,128)(2,1)}, u32[]{:S(2)}, u32[]{:S(2)}) collective-permute-start(bf16[2,4,1,32,1792]{4,3,2,1,0:T(8,128)(2,1)} %pack.144.refs_4_), channel_id=1, source_target_pairs={{0,1},{2,3},{4,5},{6,7},{1,0},{3,2},{5,4},{7,6},{8,9},{10,11},{12,... | collective-permute-start | bytes 2752520 | tf_op jit(solution)/shard_map/cond/branch_1_fun/ppermute | solution.py:411
  (76 other events, 1061.0 us)
Sparse Core Ops, SparseCore 0:
  10.2 28.9 all-gather.1
  129.9 94.5 all-reduce.5
where the time goes:
time: 547 us; the launch traced here: 544 us
  waiting for transfers between devices  207 us (38%)
  Pallas kernels  186 us (34%)
  starting transfers between devices  85.7 us (16%)
  blocking collectives  23.9 us (4%)
  local copies, waits for them, and re-layouts  22 us (4%)
  between operations  14.7 us (3%)
    ppermute x14, waiting for transfers between devices, line_exchange(): got_edge[n] = lax.ppermute(packed(pieces, after), 'roll', edge_pairs)  138 us
    pallas_call x38, Pallas kernels, pack(): pl.pallas_call(functools.partial(pack_kernel, pieces, n_in), in_specs=[sm...  97.4 us
    ppermute x12, waiting for transfers between devices, line_exchange(): got_middle[n] = lax.ppermute(packed(pieces, after), 'roll', middle_pairs)  65 us
    ppermute x14, starting transfers between devices, line_exchange(): got_edge[n] = lax.ppermute(packed(pieces, after), 'roll', edge_pairs)  37.9 us
    pallas_call x12, Pallas kernels, place_pieces(): pl.pallas_call(functools.partial(place_kernel, pieces, sources, first, bl...  37.5 us
    ppermute x12, starting transfers between devices, swap(): swapped[c, positions[0]] = lax.ppermute(packed(pieces), 'roll', swap_pairs)  32.2 us
    pallas_call x4, Pallas kernels, quantize(): pl.pallas_call(functools.partial(quantize_kernel, trains), grid=(experts,...  28.8 us
    all_to_all x1, blocking collectives, line_exchange(): lax.all_to_all(quant, 'train', split_axis=0, concat_axis=0, tiled=True)  23.9 us
  transfers between devices with their start and end apart: 43, of which 20 were waited for; matrix products, arithmetic and copies ran while one was open for 1% of the time, Pallas kernels for 33%

commit v1 on v0

--- a/solution.py
+++ b/solution.py
@@ -318,14 +318,14 @@
 EDGES = ((0, 1), (1, 0), (2, 3), (3, 2))
 
 
-def line_exchange(x_first, quants, dequant, plan, places, routed, shapes, cap):
+def line_exchange(x_first, quant_rest, dequant, plan, places, routed, shapes, cap):
     experts, blocks, trains, owners = shapes
     features = x_first.shape[-1]
     rows = BLOCK // trains
     shape = (trains, 1, rows, features)
     chunks = [(m, b) for m in range(3) for b in range(blocks)]
     count = len(chunks)
-    opens = [0 if c == 0 else 1 if m == 0 else 4 for c, (m, _) in enumerate(chunks)]
+    opens = [0 if m == 0 else 4 for m, _ in chunks]
     ride_from = 8
     middle, inwards, outwards = line_schedule(opens, experts, cap, ride_from)
     rounds = len(outwards)
@@ -337,17 +337,13 @@
     got_edge, got_middle, where = {}, {}, {}
     last = [x_first]
 
-    xs = [x_first] + [
-        lax.all_to_all(quant, "train", split_axis=0, concat_axis=0, tiled=True) for quant in quants
-    ]
+    x_rest = lax.all_to_all(quant_rest, "train", split_axis=0, concat_axis=0, tiled=True)
 
     def local(c, name):
         m, b = chunks[c]
-        if c == 0:
-            return xs[0], ("expert", places[name], 0, 0)
         if m == 0:
-            return xs[1], ("expert", places[name], 0, b - 1)
-        return xs[-1], ("expert", places[name], (m - 1) * experts, b)
+            return x_first, ("expert", places[name], 0, b)
+        return x_rest, ("expert", places[name], (m - 1) * experts, b)
 
     def packed(pieces, after=()):
         last[0] = pack(plan, shape, pieces, [last[0]] + list(after))
@@ -394,33 +390,32 @@
             choices.append(((is_outer, on_core[core]), got_edge[n], ("is", i)))
         return choices
 
-    groups = []
-    for c in range(count):
-        early = [p for p in range(4) if ready[c, p] < rounds - 4]
-        late = [p for p in range(4) if p not in early]
-        for positions in (early[:2], early[2:], late):
-            if positions:
-                groups.append((max(ready[c, p] for p in positions), c, positions))
-    groups.sort(key=lambda group: group[0])
-    swapped, swap_round, outs = {}, {}, [None, None, None]
-
-    def swap(group, n):
-        _, c, positions = group
-        pieces = [find(c, p, "mate") for p in positions]
-        swap_round[c, positions[0]] = n
-        swapped[c, positions[0]] = lax.ppermute(packed(pieces), "roll", swap_pairs)
-
-    def place(group):
-        _, c, positions = group
-        m, b = chunks[c]
-        got = swapped[c, positions[0]]
-        pieces = [find(c, p, "own") for p in positions]
-        pieces += [[((), got, ("is", n))] for n in range(len(positions))]
-        sources = [places[f"from_own{p}"] for p in positions]
-        sources += [places[f"from_mate{p}"] for p in positions]
-        outs[m], last[0] = place_pieces(
-            plan, shape, owners, pieces, sources, b, blocks, outs[m], (last[0],)
-        )
+    to_swap = sorted((ready[c, p], c, p) for c in range(count) for p in range(4))
+    to_place = []
+    outs = [None, None, None]
+
+    def swap(n, by):
+        taken = []
+        while to_swap and to_swap[0][0] <= by and len(taken) < 3:
+            taken.append(to_swap.pop(0))
+        if taken:
+            got = lax.ppermute(
+                packed([find(c, p, "mate") for _, c, p in taken]), "roll", swap_pairs
+            )
+            to_place.append((n, got, [(c, p) for _, c, p in taken]))
+        return bool(taken)
+
+    def place(got, taken):
+        for c in sorted({c for c, _ in taken}):
+            m, b = chunks[c]
+            here = [(i, p) for i, (other, p) in enumerate(taken) if other == c]
+            pieces = [find(c, p, "own") for _, p in here]
+            pieces += [[((), got, ("is", i))] for i, _ in here]
+            sources = [places[f"from_own{p}"] for _, p in here]
+            sources += [places[f"from_mate{p}"] for _, p in here]
+            outs[m], last[0] = place_pieces(
+                plan, shape, owners, pieces, sources, b, blocks, outs[m], (last[0],)
+            )
 
     ride = {}
     tokens, ids, weights = routed
@@ -472,12 +467,9 @@
         )
         last[0] = ride["mixed"]
 
-    to_swap, to_place = list(groups), []
     spare = local(0, "own")
     for n in range(rounds):
-        while to_swap and to_swap[0][0] <= n - 2:
-            to_place.append(to_swap.pop(0))
-            swap(to_place[-1], n)
+        swap(n, n - 2)
         if middle[n]:
             if where.get(("across", "ride", 0, 0), (-1,))[0] == n:
                 ride_in()
@@ -524,16 +516,14 @@
             ride_cores()
         if n == where["out", "ride", 0, 0][0] + 2:
             ride_out()
-        for group in list(to_place):
-            if swap_round[group[1], group[2][0]] <= n - 2:
-                place(group)
-                to_place.remove(group)
+        while to_place and to_place[0][0] <= n - 2:
+            place(*to_place.pop(0)[1:])
+    while to_swap:
+        swap(rounds, to_swap[0][0])
     if "mixed" not in ride:
         ride_out()
-    for group in to_swap:
-        swap(group, rounds)
-    for group in to_place + to_swap:
-        place(group)
+    for _, got, taken in to_place:
+        place(got, taken)
     return tuple(outs) + (ride["mixed"],)
 
 
@@ -804,31 +794,25 @@
     experts, hidden_rows, features = master_gate.shape
     blocks = hidden_rows // BLOCK
     if owners // CORES == 4 and CORES * tokens.shape[0] == BLOCK:
-        quant, gate = quantize(master_gate, 0, 1, trains, experts)
+        quant, gate = quantize(master_gate, 0, blocks, trains, experts)
         x_first = lax.all_to_all(quant, "train", split_axis=0, concat_axis=0, tiled=True)
         plan, places = make_plan(placement, experts, owners, (quant,))
-        quants, dequant, after = [], [gate], plan
-        if blocks > 1:
-            after, gate = quantize(master_gate, 1, blocks - 1, trains, experts, 0, None, (plan,))
-            quants.append(after)
-            dequant.append(gate)
-        rest, up = quantize(master_up, 0, blocks, trains, 2 * experts, 0, None, (after,))
+        rest, up = quantize(master_up, 0, blocks, trains, 2 * experts, 0, None, (plan,))
         rest, down = quantize(master_down, 0, blocks, trains, 2 * experts, experts, rest)
-        quants.append(rest)
-        dequant += [up, down]
+        dequant = (gate, up, down)
         routed = gather_tokens(tokens, expert_ids, gate_weights, features)
         most = min(experts, owners // 2)
         shapes = (experts, blocks, trains, owners)
 
-        def branch(cap, x_first, quants, dequant, plan, routed):
-            return line_exchange(x_first, quants, dequant, plan, places, routed, shapes, cap)
+        def branch(cap, x_first, rest, dequant, plan, routed):
+            return line_exchange(x_first, rest, dequant, plan, places, routed, shapes, cap)
 
         outs = lax.cond(
             plan[places["most"]] <= most - 1,
             functools.partial(branch, most - 1),
             functools.partial(branch, most),
             x_first,
-            quants,
+            rest,
             dequant,
             plan,
             routed,

time: 547 us -> 504 us (0.921)
  waiting for transfers between devices: 207 us -> 175 us
  blocking collectives: 23.9 us -> 0 us
  Pallas kernels: 186 us -> 204 us
  starting transfers between devices: 85.7 us -> 71.4 us
  local copies, waits for them, and re-layouts: 22 us -> 30.2 us
    ppermute x14, waiting for transfers between devices: 138 us -> 82.4 us  [line_exchange(): got_edge[n] = lax.ppermute(packed(pieces, after), 'roll', edge_pairs)]
    ppermute x14, starting transfers between devices: 37.9 us -> 11.9 us  [line_exchange(): got_edge[n] = lax.ppermute(packed(pieces, after), 'roll', edge_pairs)]
    all_to_all x1 -> x0, blocking collectives: 23.9 us -> none  [line_exchange(): lax.all_to_all(quant, 'train', split_axis=0, concat_axis=0, tiled=True)]
    psum x1, waiting for transfers between devices: 0.01 us -> 17.5 us  [ride_first(): ride['pre'] = lax.psum(pre, 'train')]
    pallas_call x12 -> x20, Pallas kernels: 37.5 us -> 54.6 us  [place_pieces(): pl.pallas_call(functools.partial(place_kernel, pieces, sources, first, bl...]
    all_to_all x1, waiting for transfers between devices: 0.01 us -> 14.9 us  [per_device(): lax.all_to_all(quant, 'train', split_axis=0, concat_axis=0, tiled=True)]
    ppermute x12 -> x13, starting transfers between devices: 32.2 us -> 40.2 us  [swap(): lax.ppermute(packed([find(c, p, 'mate') for _, c, p in taken]), 'roll', s...]
    ppermute x12, waiting for transfers between devices: 65 us -> 58.7 us  [line_exchange(): got_middle[n] = lax.ppermute(packed(pieces, after), 'roll', middle_pairs)]
  transfers between devices with their start and end apart: 43 -> 44, of which waited for: 20 -> 23; matrix products, arithmetic and copies ran while one was open for 1% -> 1% of each run, Pallas kernels for 33% -> 40%
where the time goes in v1:
time: 504 us; the launch traced here: 501 us
  Pallas kernels  204 us (40%)
  waiting for transfers between devices  175 us (35%)
  starting transfers between devices  71.4 us (14%)
  local copies, waits for them, and re-layouts  30.2 us (6%)
  between operations  14.7 us (3%)
    pallas_call x39, Pallas kernels, pack(): pl.pallas_call(functools.partial(pack_kernel, pieces, n_in), in_specs=[sm...  100 us
    ppermute x14, waiting for transfers between devices, line_exchange(): got_edge[n] = lax.ppermute(packed(pieces, after), 'roll', edge_pairs)  82.4 us
    ppermute x12, waiting for transfers between devices, line_exchange(): got_middle[n] = lax.ppermute(packed(pieces, after), 'roll', middle_pairs)  58.7 us
    pallas_call x20, Pallas kernels, place_pieces(): pl.pallas_call(functools.partial(place_kernel, pieces, sources, first, bl...  54.6 us
    ppermute x13, starting transfers between devices, swap(): lax.ppermute(packed([find(c, p, 'mate') for _, c, p in taken]), 'roll', s...  40.2 us
    pallas_call x3, Pallas kernels, quantize(): pl.pallas_call(functools.partial(quantize_kernel, trains), grid=(experts,...  26.9 us
    cond x109, local copies, waits for them, and re-layouts  23.6 us
    psum x1, waiting for transfers between devices, ride_first(): ride['pre'] = lax.psum(pre, 'train')  17.5 us
  transfers between devices with their start and end apart: 44, of which 23 were waited for; matrix products, arithmetic and copies ran while one was open for 1% of the time, Pallas kernels for 40%

profile of v1, /device:TPU:19, one launch (start us, length us, event | category | flops | bytes accessed | tf_op | source)
XLA Modules:
  0.0 500.9 jit_solution(7247455484651478526)
XLA Ops:
  9.6 8.3 %quantize.3 = (bf16[4,4,2,32,1792]{4,3,2,1,0:T(8,128)(2,1)S(1)}, bf16[4,2,128,1792]{3,2,1,0:T(8,128)(2,1)}) custom-call(f32[4,256,1792]{2,1,0:T(8,128)} %x_ref.3), custom_call_target="tpu_custom_call" | custom-call | flops 1 | bytes 1 | tf_op jit(solution)/shard_map/quantize/pallas_call | solution.py:42
  26.0 9.3 %quantize.4 = (bf16[4,8,2,32,1792]{4,3,2,1,0:T(8,128)(2,1)}, bf16[4,2,128,1792]{3,2,1,0:T(8,128)(2,1)}) custom-call(f32[4,256,1792]{2,1,0:T(8,128)} %x_ref.4, s32[29]{0:T(128)S(1)} %plan.1.refs_0_), custom_call_target="tpu_custom_call" | custom-call | flops 1 | bytes 1 | tf_op jit(solution)/shard_map/quantize/pallas_call | solution.py:42
  35.3 9.3 %quantize.5 = (bf16[4,8,2,32,1792]{4,3,2,1,0:T(8,128)(2,1)}, bf16[4,2,128,1792]{3,2,1,0:T(8,128)(2,1)}) custom-call(f32[4,256,1792]{2,1,0:T(8,128)} %x_ref.5, bf16[4,8,2,32,1792]{4,3,2,1,0:T(8,128)(2,1)} %get-tuple-element.169.refs_0_), custom_call_target="tpu_custom_call", output_to_operand_aliasing={{0}: (1, {})} | custom-call | flops 1 | bytes 1 | tf_op jit(solution)/shard_map/quantize/pallas_call | solution.py:42
  50.7 14.9 %all-to-all-done.2 = bf16[4,4,2,32,1792]{4,3,2,1,0:T(8,128)(2,1)} async-done(((bf16[4,4,2,32,1792]{4,3,2,1,0:T(8,128)(2,1)}), bf16[4,4,2,32,1792]{4,3,2,1,0:T(8,128)(2,1)}, u32[]{:S(2)}, u32[]{:S(2)}) %all-to-all-start.2) | async-done | bytes 3670048 | tf_op jit(solution)/shard_map/all_to_all | solution.py:798
  65.6 427.3 %conditional.1 = (bf16[16,32,7168]{2,1,0:T(8,128)(2,1)}, bf16[16,32,7168]{2,1,0:T(8,128)(2,1)}, bf16[16,32,7168]{2,1,0:T(8,128)(2,1)}, bf16[64,1792]{1,0:T(8,128)(2,1)}) conditional(s32[]{:T(128)} %bitcast.17, (s32[29]{0:T(128)S(1)}, bf16[4,4,2,32,1792]{4,3,2,1,0:T(8,128)(2,1)}, bf16[512,1792]{1,0:T(8,128)(2,1)}, s32[512,2]{1,0:T(8,128)S(1)}, ...), branch_computations={%region_0.2_spmd, %region_2.4_spmd} | conditional | flops 524359 | bytes 587876864 | solution.py:810
  66.3 5.8 %all-to-all-start.1 = ((bf16[4,8,2,32,1792]{4,3,2,1,0:T(8,128)(2,1)}), bf16[4,8,2,32,1792]{4,3,2,1,0:T(8,128)(2,1)}, u32[]{:S(2)}, u32[]{:S(2)}) async-start(bf16[4,8,2,32,1792]{4,3,2,1,0:T(8,128)(2,1)} %get-tuple-element.102), calls=%async_computation.1 | async-start | bytes 14680064 | tf_op jit(solution)/shard_map/cond/branch_1_fun/all_to_all | solution.py:340
  102.8 5.3 %collective-permute-done.43.refs_0_.refs_3_.refs_2_ = bf16[3,4,1,32,1792]{4,3,2,1,0:T(8,128)(2,1)S(1)} collective-permute-done((bf16[3,4,1,32,1792]{4,3,2,1,0:T(8,128)(2,1)}, bf16[3,4,1,32,1792]{4,3,2,1,0:T(8,128)(2,1)S(1)}, u32[]{:S(2)}, u32[]{:S(2)}) %collective-permute-start.43) | collective-permute-done | bytes 1376288 | tf_op jit(solution)/shard_map/cond/branch_1_fun/ppermute | solution.py:510
  116.4 21.2 %collective-permute-done.41.refs_0_.refs_3_ = bf16[3,4,1,32,1792]{4,3,2,1,0:T(8,128)(2,1)S(1)} collective-permute-done((bf16[3,4,1,32,1792]{4,3,2,1,0:T(8,128)(2,1)S(1)}, bf16[3,4,1,32,1792]{4,3,2,1,0:T(8,128)(2,1)S(1)}, u32[]{:S(2)}, u32[]{:S(2)}) %collective-permute-start.41) | collective-permute-done | bytes 1376288 | tf_op jit(solution)/shard_map/cond/branch_1_fun/ppermute | solution.py:510
  151.0 10.6 %collective-permute-done.49.refs_1_.refs_3_ = bf16[2,4,1,32,1792]{4,3,2,1,0:T(8,128)(2,1)} collective-permute-done((bf16[2,4,1,32,1792]{4,3,2,1,0:T(8,128)(2,1)}, bf16[2,4,1,32,1792]{4,3,2,1,0:T(8,128)(2,1)}, u32[]{:S(2)}, u32[]{:S(2)}) %collective-permute-start.49) | collective-permute-done | bytes 917536 | tf_op jit(solution)/shard_map/cond/branch_1_fun/ppermute | solution.py:510
  174.5 8.7 %collective-permute-start.51 = (bf16[3,4,1,32,1792]{4,3,2,1,0:T(8,128)(2,1)}, bf16[3,4,1,32,1792]{4,3,2,1,0:T(8,128)(2,1)}, u32[]{:S(2)}, u32[]{:S(2)}) collective-permute-start(bf16[3,4,1,32,1792]{4,3,2,1,0:T(8,128)(2,1)} %pack.128.refs_1_), channel_id=1, source_target_pairs={{0,1},{2,3},{4,5},{6,7},{1,0},{3,2},{5,4},{7,6},{8,9},{10,11},{12,... | collective-permute-start | bytes 4128776 | tf_op jit(solution)/shard_map/cond/branch_1_fun/ppermute | solution.py:402
  190.2 7.4 %collective-permute-done.45.refs_2_.refs_0_.refs_1_ = bf16[3,4,1,32,1792]{4,3,2,1,0:T(8,128)(2,1)} collective-permute-done((bf16[3,4,1,32,1792]{4,3,2,1,0:T(8,128)(2,1)}, bf16[3,4,1,32,1792]{4,3,2,1,0:T(8,128)(2,1)}, u32[]{:S(2)}, u32[]{:S(2)}) %collective-permute-start.45) | collective-permute-done | bytes 1376288 | tf_op jit(solution)/shard_map/cond/branch_1_fun/ppermute | solution.py:486
  203.5 17.5 %all-reduce.6.cloned.1.call-done.pre_ref = f32[512,1024]{1,0:T(8,128)} async-done(((f32[512,1024]{1,0:T(8,128)}), f32[512,1024]{1,0:T(8,128)}) %all-reduce.6.cloned.1.call-update) | async-done | bytes 2097168 | tf_op jit(solution)/shard_map/cond/branch_1_fun/psum | solution.py:431
  222.5 7.2 %mix_experts.3 = (f32[4,64,1792]{2,1,0:T(8,128)S(1)}, bf16[256,1792]{1,0:T(8,128)(2,1)S(1)}) custom-call(f32[512,1024]{1,0:T(8,128)S(1)} %copy-done.70, s32[512,2]{1,0:T(8,128)S(1)} %copy-done.104, f32[512,2]{1,0:T(8,128)} %get-tuple-element.106.weights_ref, bf16[4,2,128,1792]{3,2,1,0:T(8,128)(2,1)} %get-tuple-element.107.down_ref, ...), custom_call_target="tpu_custom_call" | custom-call | flops 1 | bytes 1 | tf_op jit(solution)/shard_map/cond/branch_1_fun/mix_experts/pallas_call | solution.py:650
  240.6 6.0 %collective-permute-start.60 = (bf16[2,4,1,32,1792]{4,3,1,0,2:T(8,128)(2,1)S(1)}, bf16[2,4,1,32,1792]{4,3,1,0,2:T(8,128)(2,1)S(1)}, u32[]{:S(2)}, u32[]{:S(2)}) collective-permute-start(bf16[2,4,1,32,1792]{4,3,1,0,2:T(8,128)(2,1)S(1)} %bitcast.36), channel_id=1, source_target_pairs={{0,1},{2,3},{4,5},{6,7},{1,0},{3,2},{5,4},{7,6},{8,9},{10,11},{12,... | collective-permute-start | bytes 2752520 | tf_op jit(solution)/shard_map/cond/branch_1_fun/ppermute | solution.py:438
  246.5 10.1 %collective-permute-done.55.refs_2_.refs_0_ = bf16[3,4,1,32,1792]{4,3,2,1,0:T(8,128)(2,1)} collective-permute-done((bf16[3,4,1,32,1792]{4,3,2,1,0:T(8,128)(2,1)}, bf16[3,4,1,32,1792]{4,3,2,1,0:T(8,128)(2,1)}, u32[]{:S(2)}, u32[]{:S(2)}) %collective-permute-start.55) | collective-permute-done | bytes 1376288 | tf_op jit(solution)/shard_map/cond/branch_1_fun/ppermute | solution.py:486
  256.6 5.5 %collective-permute-start.62 = (bf16[1,4,1,32,1792]{4,3,2,1,0:T(8,128)(2,1)S(1)}, bf16[1,4,1,32,1792]{4,3,2,1,0:T(8,128)(2,1)S(1)}, u32[]{:S(2)}, u32[]{:S(2)}) collective-permute-start(bf16[1,4,1,32,1792]{4,3,2,1,0:T(8,128)(2,1)S(1)} %pack.131.refs_1_), channel_id=1, source_target_pairs={{0,1},{2,3},{4,5},{6,7},{1,0},{3,2},{5,4},{7,6},{8,9},{10,11},{12,... | collective-permute-start | bytes 1376264 | tf_op jit(solution)/shard_map/cond/branch_1_fun/ppermute | solution.py:402
  301.9 7.7 %collective-permute-done.57.refs_1_.refs_0_.refs_3_.refs_2_ = bf16[3,4,1,32,1792]{4,3,2,1,0:T(8,128)(2,1)S(1)} collective-permute-done((bf16[3,4,1,32,1792]{4,3,2,1,0:T(8,128)(2,1)}, bf16[3,4,1,32,1792]{4,3,2,1,0:T(8,128)(2,1)S(1)}, u32[]{:S(2)}, u32[]{:S(2)}) %collective-permute-start.57) | collective-permute-done | bytes 1376288 | tf_op jit(solution)/shard_map/cond/branch_1_fun/ppermute | solution.py:510
  329.4 9.7 %collective-permute-done.64.refs_1_.refs_4_.refs_5_.refs_2_ = bf16[3,4,1,32,1792]{4,3,2,1,0:T(8,128)(2,1)S(1)} collective-permute-done((bf16[3,4,1,32,1792]{4,3,2,1,0:T(8,128)(2,1)}, bf16[3,4,1,32,1792]{4,3,2,1,0:T(8,128)(2,1)S(1)}, u32[]{:S(2)}, u32[]{:S(2)}) %collective-permute-start.64) | collective-permute-done | bytes 1376288 | tf_op jit(solution)/shard_map/cond/branch_1_fun/ppermute | solution.py:510
  362.9 5.8 %collective-permute-done.63.refs_1_.refs_4_ = bf16[3,4,1,32,1792]{4,3,2,1,0:T(8,128)(2,1)S(1)} collective-permute-done((bf16[3,4,1,32,1792]{4,3,2,1,0:T(8,128)(2,1)}, bf16[3,4,1,32,1792]{4,3,2,1,0:T(8,128)(2,1)S(1)}, u32[]{:S(2)}, u32[]{:S(2)}) %collective-permute-start.63) | collective-permute-done | bytes 1376288 | tf_op jit(solution)/shard_map/cond/branch_1_fun/ppermute | solution.py:510
  380.9 5.3 %collective-permute-start.72 = (bf16[2,4,1,32,1792]{4,3,2,1,0:T(8,128)(2,1)}, bf16[2,4,1,32,1792]{4,3,2,1,0:T(8,128)(2,1)}, u32[]{:S(2)}, u32[]{:S(2)}) collective-permute-start(bf16[2,4,1,32,1792]{4,3,2,1,0:T(8,128)(2,1)} %pack.146.refs_0_), channel_id=1, source_target_pairs={{0,1},{2,3},{4,5},{6,7},{1,0},{3,2},{5,4},{7,6},{8,9},{10,11},{12,... | collective-permute-start | bytes 2752520 | tf_op jit(solution)/shard_map/cond/branch_1_fun/ppermute | solution.py:402
  388.8 9.5 %collective-permute-done.71.refs_1_.refs_4_.refs_3_.refs_2_ = bf16[3,4,1,32,1792]{4,3,2,1,0:T(8,128)(2,1)S(1)} collective-permute-done((bf16[3,4,1,32,1792]{4,3,2,1,0:T(8,128)(2,1)S(1)}, bf16[3,4,1,32,1792]{4,3,2,1,0:T(8,128)(2,1)S(1)}, u32[]{:S(2)}, u32[]{:S(2)}) %collective-permute-start.71) | collective-permute-done | bytes 1376288 | tf_op jit(solution)/shard_map/cond/branch_1_fun/ppermute | solution.py:510
  399.9 14.0 %collective-permute-done.73.refs_0_ = bf16[4,4,1,32,1792]{4,3,2,1,0:T(8,128)(2,1)} collective-permute-done((bf16[4,4,1,32,1792]{4,3,2,1,0:T(8,128)(2,1)}, bf16[4,4,1,32,1792]{4,3,2,1,0:T(8,128)(2,1)}, u32[]{:S(2)}, u32[]{:S(2)}) %collective-permute-start.73) | collective-permute-done | bytes 1835040 | tf_op jit(solution)/shard_map/cond/branch_1_fun/ppermute | solution.py:486
  429.6 13.7 %collective-permute-done.69.refs_0_ = bf16[3,4,1,32,1792]{4,3,2,1,0:T(8,128)(2,1)} collective-permute-done((bf16[3,4,1,32,1792]{4,3,2,1,0:T(8,128)(2,1)}, bf16[3,4,1,32,1792]{4,3,2,1,0:T(8,128)(2,1)}, u32[]{:S(2)}, u32[]{:S(2)}) %collective-permute-start.69) | collective-permute-done | bytes 1376288 | tf_op jit(solution)/shard_map/cond/branch_1_fun/ppermute | solution.py:486
  463.7 9.8 %collective-permute-done.75.refs_1_ = bf16[2,4,1,32,1792]{4,3,2,1,0:T(8,128)(2,1)S(1)} collective-permute-done((bf16[2,4,1,32,1792]{4,3,2,1,0:T(8,128)(2,1)}, bf16[2,4,1,32,1792]{4,3,2,1,0:T(8,128)(2,1)S(1)}, u32[]{:S(2)}, u32[]{:S(2)}) %collective-permute-start.75) | collective-permute-done | bytes 917536 | tf_op jit(solution)/shard_map/cond/branch_1_fun/ppermute | solution.py:510
  (264 shorter events, 262.3 us)
Async XLA Ops:
  7.2 38.7 %all-gather.2.cloned.1.call-start = ((), (), s32[]{:S(2)}) async-start(), calls=%async_computation.5 | async-start | bytes 2211840 | tf_op jit(solution)/shard_map/all_gather | solution.py:784
  19.7 45.9 %all-to-all-start.2 = ((bf16[4,4,2,32,1792]{4,3,2,1,0:T(8,128)(2,1)}), bf16[4,4,2,32,1792]{4,3,2,1,0:T(8,128)(2,1)}, u32[]{:S(2)}, u32[]{:S(2)}) async-start(bf16[4,4,2,32,1792]{4,3,2,1,0:T(8,128)(2,1)} %copy-done.59), calls=%async_computation.2 | async-start | bytes 7340032 | tf_op jit(solution)/shard_map/all_to_all | solution.py:798
  66.3 101.8 %all-to-all-start.1 = ((bf16[4,8,2,32,1792]{4,3,2,1,0:T(8,128)(2,1)}), bf16[4,8,2,32,1792]{4,3,2,1,0:T(8,128)(2,1)}, u32[]{:S(2)}, u32[]{:S(2)}) async-start(bf16[4,8,2,32,1792]{4,3,2,1,0:T(8,128)(2,1)} %get-tuple-element.102), calls=%async_computation.1 | async-start | bytes 14680064 | tf_op jit(solution)/shard_map/cond/branch_1_fun/all_to_all | solution.py:340
  95.3 125.6 %all-reduce.6.cloned.1.call-start = ((), (), s32[]{:S(2)}) async-start(), calls=%async_computation.4 | async-start | bytes 4194304 | tf_op jit(solution)/shard_map/cond/branch_1_fun/psum | solution.py:431
  97.8 39.8 %collective-permute-start.41 = (bf16[3,4,1,32,1792]{4,3,2,1,0:T(8,128)(2,1)S(1)}, bf16[3,4,1,32,1792]{4,3,2,1,0:T(8,128)(2,1)S(1)}, u32[]{:S(2)}, u32[]{:S(2)}) collective-permute-start(bf16[3,4,1,32,1792]{4,3,2,1,0:T(8,128)(2,1)S(1)} %pack.122.refs_1_), channel_id=1, source_target_pairs={{0,2},{2,0},{4,6},{6,4},{1,3},{3,1},{5,7},{7,5},{8,10},{10,8},{12,... | collective-permute-start | bytes 4128776 | tf_op jit(solution)/shard_map/cond/branch_1_fun/ppermute | solution.py:510
  112.7 55.4 %collective-permute-start.48 = (bf16[3,4,1,32,1792]{4,3,2,1,0:T(8,128)(2,1)}, bf16[3,4,1,32,1792]{4,3,2,1,0:T(8,128)(2,1)S(1)}, u32[]{:S(2)}, u32[]{:S(2)}) collective-permute-start(bf16[3,4,1,32,1792]{4,3,2,1,0:T(8,128)(2,1)} %pack.124.refs_2_), channel_id=1, source_target_pairs={{2,4},{4,2},{0,1},{6,7},{3,5},{5,3},{1,0},{7,6},{10,12},{12,10},{8... | collective-permute-start | bytes 4128776 | tf_op jit(solution)/shard_map/cond/branch_1_fun/ppermute | solution.py:486
  141.1 56.5 %collective-permute-start.45 = (bf16[3,4,1,32,1792]{4,3,2,1,0:T(8,128)(2,1)}, bf16[3,4,1,32,1792]{4,3,2,1,0:T(8,128)(2,1)}, u32[]{:S(2)}, u32[]{:S(2)}) collective-permute-start(bf16[3,4,1,32,1792]{4,3,2,1,0:T(8,128)(2,1)} %pack.126.refs_2_), channel_id=1, source_target_pairs={{2,4},{4,2},{0,1},{6,7},{3,5},{5,3},{1,0},{7,6},{10,12},{12,10},{8... | collective-permute-start | bytes 4128776 | tf_op jit(solution)/shard_map/cond/branch_1_fun/ppermute | solution.py:486
  174.1 55.6 %collective-permute-start.53 = (bf16[3,4,1,32,1792]{4,3,2,1,0:T(8,128)(2,1)}, bf16[3,4,1,32,1792]{4,3,2,1,0:T(8,128)(2,1)S(1)}, u32[]{:S(2)}, u32[]{:S(2)}) collective-permute-start(bf16[3,4,1,32,1792]{4,3,2,1,0:T(8,128)(2,1)} %pack.130.refs_2_), channel_id=1, source_target_pairs={{0,2},{2,0},{4,6},{6,4},{1,3},{3,1},{5,7},{7,5},{8,10},{10,8},{12,... | collective-permute-start | bytes 4128776 | tf_op jit(solution)/shard_map/cond/branch_1_fun/ppermute | solution.py:510
  174.2 58.6 %collective-permute-start.52 = (bf16[3,4,1,32,1792]{4,3,2,1,0:T(8,128)(2,1)}, bf16[3,4,1,32,1792]{4,3,2,1,0:T(8,128)(2,1)}, u32[]{:S(2)}, u32[]{:S(2)}) collective-permute-start(bf16[3,4,1,32,1792]{4,3,2,1,0:T(8,128)(2,1)} %pack.129.refs_2_), channel_id=1, source_target_pairs={{2,4},{4,2},{0,1},{6,7},{3,5},{5,3},{1,0},{7,6},{10,12},{12,10},{8... | collective-permute-start | bytes 4128776 | tf_op jit(solution)/shard_map/cond/branch_1_fun/ppermute | solution.py:486
  174.5 65.1 %collective-permute-start.51 = (bf16[3,4,1,32,1792]{4,3,2,1,0:T(8,128)(2,1)}, bf16[3,4,1,32,1792]{4,3,2,1,0:T(8,128)(2,1)}, u32[]{:S(2)}, u32[]{:S(2)}) collective-permute-start(bf16[3,4,1,32,1792]{4,3,2,1,0:T(8,128)(2,1)} %pack.128.refs_1_), channel_id=1, source_target_pairs={{0,1},{2,3},{4,5},{6,7},{1,0},{3,2},{5,4},{7,6},{8,9},{10,11},{12,... | collective-permute-start | bytes 4128776 | tf_op jit(solution)/shard_map/cond/branch_1_fun/ppermute | solution.py:402
  203.1 53.5 %collective-permute-start.55 = (bf16[3,4,1,32,1792]{4,3,2,1,0:T(8,128)(2,1)}, bf16[3,4,1,32,1792]{4,3,2,1,0:T(8,128)(2,1)}, u32[]{:S(2)}, u32[]{:S(2)}) collective-permute-start(bf16[3,4,1,32,1792]{4,3,2,1,0:T(8,128)(2,1)} %pack.132.refs_2_), channel_id=1, source_target_pairs={{2,4},{4,2},{0,1},{6,7},{3,5},{5,3},{1,0},{7,6},{10,12},{12,10},{8... | collective-permute-start | bytes 4128776 | tf_op jit(solution)/shard_map/cond/branch_1_fun/ppermute | solution.py:486
  238.3 45.3 %collective-permute-start.61 = (bf16[3,4,1,32,1792]{4,3,2,1,0:T(8,128)(2,1)}, bf16[3,4,1,32,1792]{4,3,2,1,0:T(8,128)(2,1)S(1)}, u32[]{:S(2)}, u32[]{:S(2)}) collective-permute-start(bf16[3,4,1,32,1792]{4,3,2,1,0:T(8,128)(2,1)} %pack.136.refs_4_), channel_id=1, source_target_pairs={{0,2},{2,0},{4,6},{6,4},{1,3},{3,1},{5,7},{7,5},{8,10},{10,8},{12,... | collective-permute-start | bytes 4128776 | tf_op jit(solution)/shard_map/cond/branch_1_fun/ppermute | solution.py:510
  239.6 46.5 %collective-permute-start.59 = (bf16[3,4,1,32,1792]{4,3,2,1,0:T(8,128)(2,1)}, bf16[3,4,1,32,1792]{4,3,2,1,0:T(8,128)(2,1)}, u32[]{:S(2)}, u32[]{:S(2)}) collective-permute-start(bf16[3,4,1,32,1792]{4,3,2,1,0:T(8,128)(2,1)} %pack.135.refs_2_), channel_id=1, source_target_pairs={{2,4},{4,2},{0,1},{6,7},{3,5},{5,3},{1,0},{7,6},{10,12},{12,10},{8... | collective-permute-start | bytes 4128776 | tf_op jit(solution)/shard_map/cond/branch_1_fun/ppermute | solution.py:486
  239.6 54.3 %collective-permute-start.58 = (bf16[3,4,1,32,1792]{4,3,2,1,0:T(8,128)(2,1)}, bf16[3,4,1,32,1792]{4,3,2,1,0:T(8,128)(2,1)}, u32[]{:S(2)}, u32[]{:S(2)}) collective-permute-start(bf16[3,4,1,32,1792]{4,3,2,1,0:T(8,128)(2,1)} %pack.134.refs_1_), channel_id=1, source_target_pairs={{0,1},{2,3},{4,5},{6,7},{1,0},{3,2},{5,4},{7,6},{8,9},{10,11},{12,... | collective-permute-start | bytes 4128776 | tf_op jit(solution)/shard_map/cond/branch_1_fun/ppermute | solution.py:402
  292.2 47.0 %collective-permute-start.64 = (bf16[3,4,1,32,1792]{4,3,2,1,0:T(8,128)(2,1)}, bf16[3,4,1,32,1792]{4,3,2,1,0:T(8,128)(2,1)S(1)}, u32[]{:S(2)}, u32[]{:S(2)}) collective-permute-start(bf16[3,4,1,32,1792]{4,3,2,1,0:T(8,128)(2,1)} %pack.142.refs_3_), channel_id=1, source_target_pairs={{0,2},{2,0},{4,6},{6,4},{1,3},{3,1},{5,7},{7,5},{8,10},{10,8},{12,... | collective-permute-start | bytes 4128776 | tf_op jit(solution)/shard_map/cond/branch_1_fun/ppermute | solution.py:510
  293.9 51.0 %collective-permute-start.66 = (bf16[3,4,1,32,1792]{4,3,2,1,0:T(8,128)(2,1)}, bf16[3,4,1,32,1792]{4,3,2,1,0:T(8,128)(2,1)S(1)}, u32[]{:S(2)}, u32[]{:S(2)}) collective-permute-start(bf16[3,4,1,32,1792]{4,3,2,1,0:T(8,128)(2,1)} %copy-done.69), channel_id=1, source_target_pairs={{2,4},{4,2},{0,1},{6,7},{3,5},{5,3},{1,0},{7,6},{10,12},{12,10},{8... | collective-permute-start | bytes 4128776 | tf_op jit(solution)/shard_map/cond/branch_1_fun/ppermute | solution.py:486
  321.3 47.3 %collective-permute-start.63 = (bf16[3,4,1,32,1792]{4,3,2,1,0:T(8,128)(2,1)}, bf16[3,4,1,32,1792]{4,3,2,1,0:T(8,128)(2,1)S(1)}, u32[]{:S(2)}, u32[]{:S(2)}) collective-permute-start(bf16[3,4,1,32,1792]{4,3,2,1,0:T(8,128)(2,1)} %pack.145.refs_3_), channel_id=1, source_target_pairs={{0,2},{2,0},{4,6},{6,4},{1,3},{3,1},{5,7},{7,5},{8,10},{10,8},{12,... | collective-permute-start | bytes 4128776 | tf_op jit(solution)/shard_map/cond/branch_1_fun/ppermute | solution.py:510
  321.4 53.1 %collective-permute-start.68 = (bf16[3,4,1,32,1792]{4,3,2,1,0:T(8,128)(2,1)}, bf16[3,4,1,32,1792]{4,3,2,1,0:T(8,128)(2,1)S(1)}, u32[]{:S(2)}, u32[]{:S(2)}) collective-permute-start(bf16[3,4,1,32,1792]{4,3,2,1,0:T(8,128)(2,1)} %pack.144.refs_2_), channel_id=1, source_target_pairs={{2,4},{4,2},{0,1},{6,7},{3,5},{5,3},{1,0},{7,6},{10,12},{12,10},{8... | collective-permute-start | bytes 4128776 | tf_op jit(solution)/shard_map/cond/branch_1_fun/ppermute | solution.py:486
  348.9 64.9 %collective-permute-start.73 = (bf16[4,4,1,32,1792]{4,3,2,1,0:T(8,128)(2,1)}, bf16[4,4,1,32,1792]{4,3,2,1,0:T(8,128)(2,1)}, u32[]{:S(2)}, u32[]{:S(2)}) collective-permute-start(bf16[4,4,1,32,1792]{4,3,2,1,0:T(8,128)(2,1)} %pack.147.refs_3_), channel_id=1, source_target_pairs={{2,4},{4,2},{0,1},{6,7},{3,5},{5,3},{1,0},{7,6},{10,12},{12,10},{8... | collective-permute-start | bytes 5505032 | tf_op jit(solution)/shard_map/cond/branch_1_fun/ppermute | solution.py:486
  353.1 45.1 %collective-permute-start.71 = (bf16[3,4,1,32,1792]{4,3,2,1,0:T(8,128)(2,1)S(1)}, bf16[3,4,1,32,1792]{4,3,2,1,0:T(8,128)(2,1)S(1)}, u32[]{:S(2)}, u32[]{:S(2)}) collective-permute-start(bf16[3,4,1,32,1792]{4,3,2,1,0:T(8,128)(2,1)S(1)} %pack.148.refs_3_), channel_id=1, source_target_pairs={{0,2},{2,0},{4,6},{6,4},{1,3},{3,1},{5,7},{7,5},{8,10},{10,8},{12,... | collective-permute-start | bytes 4128776 | tf_op jit(solution)/shard_map/cond/branch_1_fun/ppermute | solution.py:510
  380.5 47.0 %collective-permute-start.70 = (bf16[3,4,1,32,1792]{4,3,2,1,0:T(8,128)(2,1)}, bf16[3,4,1,32,1792]{4,3,2,1,0:T(8,128)(2,1)}, u32[]{:S(2)}, u32[]{:S(2)}) collective-permute-start(bf16[3,4,1,32,1792]{4,3,2,1,0:T(8,128)(2,1)} %pack.151.refs_3_), channel_id=1, source_target_pairs={{0,2},{2,0},{4,6},{6,4},{1,3},{3,1},{5,7},{7,5},{8,10},{10,8},{12,... | collective-permute-start | bytes 4128776 | tf_op jit(solution)/shard_map/cond/branch_1_fun/ppermute | solution.py:510
  380.5 62.8 %collective-permute-start.69 = (bf16[3,4,1,32,1792]{4,3,2,1,0:T(8,128)(2,1)}, bf16[3,4,1,32,1792]{4,3,2,1,0:T(8,128)(2,1)}, u32[]{:S(2)}, u32[]{:S(2)}) collective-permute-start(bf16[3,4,1,32,1792]{4,3,2,1,0:T(8,128)(2,1)} %pack.150.refs_3_), channel_id=1, source_target_pairs={{2,4},{4,2},{0,1},{6,7},{3,5},{5,3},{1,0},{7,6},{10,12},{12,10},{8... | collective-permute-start | bytes 4128776 | tf_op jit(solution)/shard_map/cond/branch_1_fun/ppermute | solution.py:486
  380.9 40.5 %collective-permute-start.72 = (bf16[2,4,1,32,1792]{4,3,2,1,0:T(8,128)(2,1)}, bf16[2,4,1,32,1792]{4,3,2,1,0:T(8,128)(2,1)}, u32[]{:S(2)}, u32[]{:S(2)}) collective-permute-start(bf16[2,4,1,32,1792]{4,3,2,1,0:T(8,128)(2,1)} %pack.146.refs_0_), channel_id=1, source_target_pairs={{0,1},{2,3},{4,5},{6,7},{1,0},{3,2},{5,4},{7,6},{8,9},{10,11},{12,... | collective-permute-start | bytes 2752520 | tf_op jit(solution)/shard_map/cond/branch_1_fun/ppermute | solution.py:402
  398.2 50.8 %collective-permute-start.67 = (bf16[3,4,1,32,1792]{4,3,2,1,0:T(8,128)(2,1)}, bf16[3,4,1,32,1792]{4,3,2,1,0:T(8,128)(2,1)}, u32[]{:S(2)}, u32[]{:S(2)}) collective-permute-start(bf16[3,4,1,32,1792]{4,3,2,1,0:T(8,128)(2,1)} %pack.149.refs_1_), channel_id=1, source_target_pairs={{0,1},{2,3},{4,5},{6,7},{1,0},{3,2},{5,4},{7,6},{8,9},{10,11},{12,... | collective-permute-start | bytes 4128776 | tf_op jit(solution)/shard_map/cond/branch_1_fun/ppermute | solution.py:402
  (76 other events, 1089.3 us)
Sparse Core Ops, SparseCore 0:
  10.2 29.0 all-gather.1
  151.2 69.7 all-reduce.5

commit v2 on v1

--- a/solution.py
+++ b/solution.py
@@ -325,7 +325,7 @@
     shape = (trains, 1, rows, features)
     chunks = [(m, b) for m in range(3) for b in range(blocks)]
     count = len(chunks)
-    opens = [0 if m == 0 else 4 for m, _ in chunks]
+    opens = [(0, 3, 4)[m] for m, _ in chunks]
     ride_from = 8
     middle, inwards, outwards = line_schedule(opens, experts, cap, ride_from)
     rounds = len(outwards)
@@ -337,13 +337,14 @@
     got_edge, got_middle, where = {}, {}, {}
     last = [x_first]
 
-    x_rest = lax.all_to_all(quant_rest, "train", split_axis=0, concat_axis=0, tiled=True)
+    xs = [x_first] + [
+        lax.all_to_all(quant, "train", split_axis=0, concat_axis=0, tiled=True)
+        for quant in quant_rest
+    ]
 
     def local(c, name):
         m, b = chunks[c]
-        if m == 0:
-            return x_first, ("expert", places[name], 0, b)
-        return x_rest, ("expert", places[name], (m - 1) * experts, b)
+        return xs[m], ("expert", places[name], 0, b)
 
     def packed(pieces, after=()):
         last[0] = pack(plan, shape, pieces, [last[0]] + list(after))
@@ -519,7 +520,11 @@
         while to_place and to_place[0][0] <= n - 2:
             place(*to_place.pop(0)[1:])
     while to_swap:
+        early = list(to_place)
+        del to_place[:]
         swap(rounds, to_swap[0][0])
+        for _, got, taken in early:
+            place(got, taken)
     if "mixed" not in ride:
         ride_out()
     for _, got, taken in to_place:
@@ -797,8 +802,9 @@
         quant, gate = quantize(master_gate, 0, blocks, trains, experts)
         x_first = lax.all_to_all(quant, "train", split_axis=0, concat_axis=0, tiled=True)
         plan, places = make_plan(placement, experts, owners, (quant,))
-        rest, up = quantize(master_up, 0, blocks, trains, 2 * experts, 0, None, (plan,))
-        rest, down = quantize(master_down, 0, blocks, trains, 2 * experts, experts, rest)
+        rest_up, up = quantize(master_up, 0, blocks, trains, experts, 0, None, (plan,))
+        rest_down, down = quantize(master_down, 0, blocks, trains, experts, 0, None, (rest_up,))
+        rest = (rest_up, rest_down)
         dequant = (gate, up, down)
         routed = gather_tokens(tokens, expert_ids, gate_weights, features)
         most = min(experts, owners // 2)

time: 504 us -> 606 us (1.20)
  waiting for transfers between devices: 175 us -> 268 us
  starting transfers between devices: 71.4 us -> 89.2 us
  Pallas kernels: 204 us -> 197 us
    ppermute x12, waiting for transfers between devices: 58.7 us -> 112 us  [line_exchange(): got_middle[n] = lax.ppermute(packed(pieces, after), 'roll', middle_pairs)]
    ppermute x14, waiting for transfers between devices: 82.4 us -> 126 us  [line_exchange(): got_edge[n] = lax.ppermute(packed(pieces, after), 'roll', edge_pairs)]
    psum x1, waiting for transfers between devices: 17.5 us -> 0.01 us  [ride_first(): ride['pre'] = lax.psum(pre, 'train')]
    all_to_all x1 -> x2, waiting for transfers between devices: 0.01 us -> 12.7 us  [line_exchange(): lax.all_to_all(quant, 'train', split_axis=0, concat_axis=0, tiled=True)]
    ppermute x14, starting transfers between devices: 11.9 us -> 19.4 us  [line_exchange(): got_edge[n] = lax.ppermute(packed(pieces, after), 'roll', edge_pairs)]
    ppermute x1, starting transfers between devices: 5.95 us -> 12.3 us  [ride_mix(): ride['swapped'] = lax.ppermute(going, 'roll', swap_pairs)]
    pallas_call x39 -> x40, Pallas kernels: 100 us -> 96.5 us  [pack(): pl.pallas_call(functools.partial(pack_kernel, pieces, n_in), in_specs=[sm...]
    cond x109 -> x101, local copies, waits for them, and re-layouts: 23.6 us -> 21.2 us
  transfers between devices with their start and end apart: 44 -> 46, of which waited for: 23 -> 21; matrix products, arithmetic and copies ran while one was open for 1% -> 1% of each run, Pallas kernels for 40% -> 32%
where the time goes in v2:
time: 606 us; the launch traced here: 603 us
  waiting for transfers between devices  268 us (44%)
  Pallas kernels  197 us (33%)
  starting transfers between devices  89.2 us (15%)
  local copies, waits for them, and re-layouts  27.8 us (5%)
  between operations  14.7 us (2%)
    ppermute x14, waiting for transfers between devices, line_exchange(): got_edge[n] = lax.ppermute(packed(pieces, after), 'roll', edge_pairs)  126 us
    ppermute x12, waiting for transfers between devices, line_exchange(): got_middle[n] = lax.ppermute(packed(pieces, after), 'roll', middle_pairs)  112 us
    pallas_call x40, Pallas kernels, pack(): pl.pallas_call(functools.partial(pack_kernel, pieces, n_in), in_specs=[sm...  96.5 us
    pallas_call x21, Pallas kernels, place_pieces(): pl.pallas_call(functools.partial(place_kernel, pieces, sources, first, bl...  53.6 us
    ppermute x14, starting transfers between devices, swap(): lax.ppermute(packed([find(c, p, 'mate') for _, c, p in taken]), 'roll', s...  39 us
    pallas_call x3, Pallas kernels, quantize(): pl.pallas_call(functools.partial(quantize_kernel, trains), grid=(experts,...  26.3 us
    cond x101, local copies, waits for them, and re-layouts  21.2 us
    ppermute x14, starting transfers between devices, line_exchange(): got_edge[n] = lax.ppermute(packed(pieces, after), 'roll', edge_pairs)  19.4 us
  transfers between devices with their start and end apart: 46, of which 21 were waited for; matrix products, arithmetic and copies ran while one was open for 1% of the time, Pallas kernels for 32%

profile of v2, /device:TPU:19, one launch (start us, length us, event | category | flops | bytes accessed | tf_op | source)
XLA Modules:
  0.0 602.8 jit_solution(6495827967799887594)
XLA Ops:
  9.6 8.3 %quantize.3 = (bf16[4,4,2,32,1792]{4,3,2,1,0:T(8,128)(2,1)S(1)}, bf16[4,2,128,1792]{3,2,1,0:T(8,128)(2,1)}) custom-call(f32[4,256,1792]{2,1,0:T(8,128)} %x_ref.3), custom_call_target="tpu_custom_call" | custom-call | flops 1 | bytes 1 | tf_op jit(solution)/shard_map/quantize/pallas_call | solution.py:42
  26.0 8.3 %quantize.4 = (bf16[4,4,2,32,1792]{4,3,2,1,0:T(8,128)(2,1)S(1)}, bf16[4,2,128,1792]{3,2,1,0:T(8,128)(2,1)}) custom-call(f32[4,256,1792]{2,1,0:T(8,128)} %x_ref.4, s32[29]{0:T(128)S(1)} %plan.1.refs_0_), custom_call_target="tpu_custom_call" | custom-call | flops 1 | bytes 1 | tf_op jit(solution)/shard_map/quantize/pallas_call | solution.py:42
  34.3 9.7 %quantize.5 = (bf16[4,4,2,32,1792]{4,3,2,1,0:T(8,128)(2,1)}, bf16[4,2,128,1792]{3,2,1,0:T(8,128)(2,1)}) custom-call(f32[4,256,1792]{2,1,0:T(8,128)} %x_ref.5, bf16[4,4,2,32,1792]{4,3,2,1,0:T(8,128)(2,1)S(1)} %get-tuple-element.175.refs_0_), custom_call_target="tpu_custom_call" | custom-call | flops 1 | bytes 1 | tf_op jit(solution)/shard_map/quantize/pallas_call | solution.py:42
  50.0 15.5 %all-to-all-done.4 = bf16[4,4,2,32,1792]{4,3,2,1,0:T(8,128)(2,1)} async-done(((bf16[4,4,2,32,1792]{4,3,2,1,0:T(8,128)(2,1)}), bf16[4,4,2,32,1792]{4,3,2,1,0:T(8,128)(2,1)}, u32[]{:S(2)}, u32[]{:S(2)}) %all-to-all-start.4) | async-done | bytes 3670048 | tf_op jit(solution)/shard_map/all_to_all | solution.py:803
  65.6 529.2 %conditional.1 = (bf16[16,32,7168]{2,1,0:T(8,128)(2,1)}, bf16[16,32,7168]{2,1,0:T(8,128)(2,1)}, bf16[16,32,7168]{2,1,0:T(8,128)(2,1)}, bf16[64,1792]{1,0:T(8,128)(2,1)}) conditional(s32[]{:T(128)} %bitcast.17, (s32[29]{0:T(128)S(1)}, bf16[4,4,2,32,1792]{4,3,2,1,0:T(8,128)(2,1)}, bf16[512,1792]{1,0:T(8,128)(2,1)}, s32[512,2]{1,0:T(8,128)S(1)}, ...), branch_computations={%region_0.2_spmd, %region_2.4_spmd} | conditional | flops 524358 | bytes 509873120 | solution.py:816
  98.1 12.7 %all-to-all-done.1.refs_1_.refs_0_.refs_2_ = bf16[4,4,2,32,1792]{4,3,2,1,0:T(8,128)(2,1)} async-done(((bf16[4,4,2,32,1792]{4,3,2,1,0:T(8,128)(2,1)}), bf16[4,4,2,32,1792]{4,3,2,1,0:T(8,128)(2,1)}, u32[]{:S(2)}, u32[]{:S(2)}) %all-to-all-start.1) | async-done | bytes 3670048 | tf_op jit(solution)/shard_map/cond/branch_0_fun/all_to_all | solution.py:341
  110.8 5.9 all-to-all-start
  125.4 30.8 %collective-permute-done.refs_0_.refs_3_ = bf16[4,4,1,32,1792]{4,3,2,1,0:T(8,128)(2,1)} collective-permute-done((bf16[4,4,1,32,1792]{4,3,2,1,0:T(8,128)(2,1)}, bf16[4,4,1,32,1792]{4,3,2,1,0:T(8,128)(2,1)}, u32[]{:S(2)}, u32[]{:S(2)}) %collective-permute-start) | collective-permute-done | bytes 1835040 | tf_op jit(solution)/shard_map/cond/branch_0_fun/ppermute | solution.py:511
  170.4 50.5 %collective-permute-done.8.refs_1_.refs_3_ = bf16[2,4,1,32,1792]{4,3,2,1,0:T(8,128)(2,1)S(1)} collective-permute-done((bf16[2,4,1,32,1792]{4,3,2,1,0:T(8,128)(2,1)}, bf16[2,4,1,32,1792]{4,3,2,1,0:T(8,128)(2,1)S(1)}, u32[]{:S(2)}, u32[]{:S(2)}) %collective-permute-start.8) | collective-permute-done | bytes 917536 | tf_op jit(solution)/shard_map/cond/branch_0_fun/ppermute | solution.py:511
  245.3 6.6 %collective-permute-start.9 = (bf16[4,4,1,32,1792]{4,3,2,1,0:T(8,128)(2,1)}, bf16[4,4,1,32,1792]{4,3,2,1,0:T(8,128)(2,1)}, u32[]{:S(2)}, u32[]{:S(2)}) collective-permute-start(bf16[4,4,1,32,1792]{4,3,2,1,0:T(8,128)(2,1)} %pack.94.refs_0_), channel_id=1, source_target_pairs={{0,2},{2,0},{4,6},{6,4},{1,3},{3,1},{5,7},{7,5},{8,10},{10,8},{12,... | collective-permute-start | bytes 5505032 | tf_op jit(solution)/shard_map/cond/branch_0_fun/ppermute | solution.py:511
  252.6 8.1 %mix_experts.2 = (f32[4,64,1792]{2,1,0:T(8,128)S(1)}, bf16[256,1792]{1,0:T(8,128)(2,1)}) custom-call(f32[512,1024]{1,0:T(8,128)} %all-reduce.4.cloned.1.call-done.pre_ref, s32[512,2]{1,0:T(8,128)S(1)} %get-tuple-element.43.ids_ref, f32[512,2]{1,0:T(8,128)} %get-tuple-element.51.weights_ref, bf16[4,2,128,1792]{3,2,1,0:T(8,128)(2,1)} %get-tuple-element.52.down_ref, ...), custom_call_target="tpu_custom_call" | custom-call | flops 1 | bytes 1 | tf_op jit(solution)/shard_map/cond/branch_0_fun/mix_experts/pallas_call | solution.py:655
  269.6 5.6 collective-permute-done.11.refs_2_.refs_0_.refs_1_
  281.2 6.8 %collective-permute-start.22 = (bf16[3,4,1,32,1792]{4,3,2,1,0:T(8,128)(2,1)}, bf16[3,4,1,32,1792]{4,3,2,1,0:T(8,128)(2,1)}, u32[]{:S(2)}, u32[]{:S(2)}) collective-permute-start(bf16[3,4,1,32,1792]{4,3,2,1,0:T(8,128)(2,1)} %pack.92.refs_1_), channel_id=1, source_target_pairs={{0,1},{2,3},{4,5},{6,7},{1,0},{3,2},{5,4},{7,6},{8,9},{10,11},{12,... | collective-permute-start | bytes 4128776 | tf_op jit(solution)/shard_map/cond/branch_0_fun/ppermute | solution.py:403
  288.0 18.2 %collective-permute-done.9.refs_2_.refs_0_.refs_3_.refs_1_ = bf16[4,4,1,32,1792]{4,3,2,1,0:T(8,128)(2,1)} collective-permute-done((bf16[4,4,1,32,1792]{4,3,2,1,0:T(8,128)(2,1)}, bf16[4,4,1,32,1792]{4,3,2,1,0:T(8,128)(2,1)}, u32[]{:S(2)}, u32[]{:S(2)}) %collective-permute-start.9) | collective-permute-done | bytes 1835040 | tf_op jit(solution)/shard_map/cond/branch_0_fun/ppermute | solution.py:511
  306.2 12.3 %collective-permute-start.20 = (bf16[2,4,1,32,1792]{4,3,1,0,2:T(8,128)(2,1)}, bf16[2,4,1,32,1792]{4,3,1,0,2:T(8,128)(2,1)S(1)}, u32[]{:S(2)}, u32[]{:S(2)}) collective-permute-start(bf16[2,4,1,32,1792]{4,3,1,0,2:T(8,128)(2,1)} %bitcast), channel_id=1, source_target_pairs={{0,1},{2,3},{4,5},{6,7},{1,0},{3,2},{5,4},{7,6},{8,9},{10,11},{12,... | collective-permute-start | bytes 2752520 | tf_op jit(solution)/shard_map/cond/branch_0_fun/ppermute | solution.py:439
  340.0 5.4 collective-permute-done.21.refs_2_.refs_0_.refs_3_.refs_1_
  381.4 11.7 %collective-permute-done.16.refs_2_.refs_0_ = bf16[4,4,1,32,1792]{4,3,2,1,0:T(8,128)(2,1)S(1)} collective-permute-done((bf16[4,4,1,32,1792]{4,3,2,1,0:T(8,128)(2,1)}, bf16[4,4,1,32,1792]{4,3,2,1,0:T(8,128)(2,1)S(1)}, u32[]{:S(2)}, u32[]{:S(2)}) %collective-permute-start.16) | collective-permute-done | bytes 1835040 | tf_op jit(solution)/shard_map/cond/branch_0_fun/ppermute | solution.py:487
  413.7 18.7 %collective-permute-done.26.refs_3_.refs_0_ = bf16[4,4,1,32,1792]{4,3,2,1,0:T(8,128)(2,1)S(1)} collective-permute-done((bf16[4,4,1,32,1792]{4,3,2,1,0:T(8,128)(2,1)}, bf16[4,4,1,32,1792]{4,3,2,1,0:T(8,128)(2,1)S(1)}, u32[]{:S(2)}, u32[]{:S(2)}) %collective-permute-start.26) | collective-permute-done | bytes 1835040 | tf_op jit(solution)/shard_map/cond/branch_0_fun/ppermute | solution.py:487
  445.6 7.1 %collective-permute-done.24.refs_1_.refs_3_ = bf16[2,4,1,32,1792]{4,3,2,1,0:T(8,128)(2,1)} collective-permute-done((bf16[2,4,1,32,1792]{4,3,2,1,0:T(8,128)(2,1)}, bf16[2,4,1,32,1792]{4,3,2,1,0:T(8,128)(2,1)}, u32[]{:S(2)}, u32[]{:S(2)}) %collective-permute-start.24) | collective-permute-done | bytes 917536 | tf_op jit(solution)/shard_map/cond/branch_0_fun/ppermute | solution.py:511
  453.8 17.9 %collective-permute-done.23.refs_2_.refs_0_ = bf16[4,4,1,32,1792]{4,3,2,1,0:T(8,128)(2,1)S(1)} collective-permute-done((bf16[4,4,1,32,1792]{4,3,2,1,0:T(8,128)(2,1)}, bf16[4,4,1,32,1792]{4,3,2,1,0:T(8,128)(2,1)S(1)}, u32[]{:S(2)}, u32[]{:S(2)}) %collective-permute-start.23) | collective-permute-done | bytes 1835040 | tf_op jit(solution)/shard_map/cond/branch_0_fun/ppermute | solution.py:487
  492.7 28.2 %collective-permute-done.30.refs_0_ = bf16[5,4,1,32,1792]{4,3,2,1,0:T(8,128)(2,1)S(1)} collective-permute-done((bf16[5,4,1,32,1792]{4,3,2,1,0:T(8,128)(2,1)}, bf16[5,4,1,32,1792]{4,3,2,1,0:T(8,128)(2,1)S(1)}, u32[]{:S(2)}, u32[]{:S(2)}) %collective-permute-start.30) | collective-permute-done | bytes 2293792 | tf_op jit(solution)/shard_map/cond/branch_0_fun/ppermute | solution.py:487
  524.7 5.5 collective-permute-start.29
  535.0 25.3 %collective-permute-done.37.refs_0_ = bf16[4,4,1,32,1792]{4,3,2,1,0:T(8,128)(2,1)} collective-permute-done((bf16[4,4,1,32,1792]{4,3,2,1,0:T(8,128)(2,1)}, bf16[4,4,1,32,1792]{4,3,2,1,0:T(8,128)(2,1)}, u32[]{:S(2)}, u32[]{:S(2)}) %collective-permute-start.37) | collective-permute-done | bytes 1835040 | tf_op jit(solution)/shard_map/cond/branch_0_fun/ppermute | solution.py:487
  574.9 6.5 %collective-permute-done.38.refs_1_ = bf16[2,4,1,32,1792]{4,3,2,1,0:T(8,128)(2,1)S(1)} collective-permute-done((bf16[2,4,1,32,1792]{4,3,2,1,0:T(8,128)(2,1)S(1)}, bf16[2,4,1,32,1792]{4,3,2,1,0:T(8,128)(2,1)S(1)}, u32[]{:S(2)}, u32[]{:S(2)}) %collective-permute-start.38) | collective-permute-done | bytes 917536 | tf_op jit(solution)/shard_map/cond/branch_0_fun/ppermute | solution.py:511
  (264 shorter events, 260.9 us)
Async XLA Ops:
  19.7 45.9 %all-to-all-start.4 = ((bf16[4,4,2,32,1792]{4,3,2,1,0:T(8,128)(2,1)}), bf16[4,4,2,32,1792]{4,3,2,1,0:T(8,128)(2,1)}, u32[]{:S(2)}, u32[]{:S(2)}) async-start(bf16[4,4,2,32,1792]{4,3,2,1,0:T(8,128)(2,1)} %copy-done.41), calls=%async_computation.4 | async-start | bytes 7340032 | tf_op jit(solution)/shard_map/all_to_all | solution.py:803
  65.6 45.3 %all-to-all-start.1 = ((bf16[4,4,2,32,1792]{4,3,2,1,0:T(8,128)(2,1)}), bf16[4,4,2,32,1792]{4,3,2,1,0:T(8,128)(2,1)}, u32[]{:S(2)}, u32[]{:S(2)}) async-start(bf16[4,4,2,32,1792]{4,3,2,1,0:T(8,128)(2,1)} %get-tuple-element.47), calls=%async_computation.1 | async-start | bytes 7340032 | tf_op jit(solution)/shard_map/cond/branch_0_fun/all_to_all | solution.py:341
  95.9 60.3 %collective-permute-start = (bf16[4,4,1,32,1792]{4,3,2,1,0:T(8,128)(2,1)}, bf16[4,4,1,32,1792]{4,3,2,1,0:T(8,128)(2,1)}, u32[]{:S(2)}, u32[]{:S(2)}) collective-permute-start(bf16[4,4,1,32,1792]{4,3,2,1,0:T(8,128)(2,1)} %pack.82.refs_2_), channel_id=1, source_target_pairs={{0,2},{2,0},{4,6},{6,4},{1,3},{3,1},{5,7},{7,5},{8,10},{10,8},{12,... | collective-permute-start | bytes 5505032 | tf_op jit(solution)/shard_map/cond/branch_0_fun/ppermute | solution.py:511
  97.9 60.1 %collective-permute-start.3 = (bf16[4,4,1,32,1792]{4,3,2,1,0:T(8,128)(2,1)}, bf16[4,4,1,32,1792]{4,3,2,1,0:T(8,128)(2,1)}, u32[]{:S(2)}, u32[]{:S(2)}) collective-permute-start(bf16[4,4,1,32,1792]{4,3,2,1,0:T(8,128)(2,1)} %pack.81.refs_1_), channel_id=1, source_target_pairs={{2,4},{4,2},{0,1},{6,7},{3,5},{5,3},{1,0},{7,6},{10,12},{12,10},{8... | collective-permute-start | bytes 5505032 | tf_op jit(solution)/shard_map/cond/branch_0_fun/ppermute | solution.py:487
  110.8 131.6 %all-to-all-start = ((bf16[4,4,2,32,1792]{4,3,2,1,0:T(8,128)(2,1)}), bf16[4,4,2,32,1792]{4,3,2,1,0:T(8,128)(2,1)}, u32[]{:S(2)}, u32[]{:S(2)}) async-start(bf16[4,4,2,32,1792]{4,3,2,1,0:T(8,128)(2,1)} %get-tuple-element.46), calls=%async_computation | async-start | bytes 7340032 | tf_op jit(solution)/shard_map/cond/branch_0_fun/all_to_all | solution.py:341
  116.7 135.8 %all-reduce.4.cloned.1.call-start = ((), (), s32[]{:S(2)}) async-start(), calls=%async_computation.5 | async-start | bytes 4194304 | tf_op jit(solution)/shard_map/cond/branch_0_fun/psum | solution.py:432
  122.7 100.0 %collective-permute-start.7 = (bf16[4,4,1,32,1792]{4,3,2,1,0:T(8,128)(2,1)}, bf16[4,4,1,32,1792]{4,3,2,1,0:T(8,128)(2,1)}, u32[]{:S(2)}, u32[]{:S(2)}) collective-permute-start(bf16[4,4,1,32,1792]{4,3,2,1,0:T(8,128)(2,1)} %pack.84.refs_2_), channel_id=1, source_target_pairs={{2,4},{4,2},{0,1},{6,7},{3,5},{5,3},{1,0},{7,6},{10,12},{12,10},{8... | collective-permute-start | bytes 5505032 | tf_op jit(solution)/shard_map/cond/branch_0_fun/ppermute | solution.py:487
  163.9 72.9 %collective-permute-start.5 = (bf16[4,4,1,32,1792]{4,3,2,1,0:T(8,128)(2,1)}, bf16[4,4,1,32,1792]{4,3,2,1,0:T(8,128)(2,1)}, u32[]{:S(2)}, u32[]{:S(2)}) collective-permute-start(bf16[4,4,1,32,1792]{4,3,2,1,0:T(8,128)(2,1)} %pack.88.refs_2_), channel_id=1, source_target_pairs={{0,2},{2,0},{4,6},{6,4},{1,3},{3,1},{5,7},{7,5},{8,10},{10,8},{12,... | collective-permute-start | bytes 5505032 | tf_op jit(solution)/shard_map/cond/branch_0_fun/ppermute | solution.py:511
  164.5 74.9 %collective-permute-start.4 = (bf16[4,4,1,32,1792]{4,3,2,1,0:T(8,128)(2,1)}, bf16[4,4,1,32,1792]{4,3,2,1,0:T(8,128)(2,1)}, u32[]{:S(2)}, u32[]{:S(2)}) collective-permute-start(bf16[4,4,1,32,1792]{4,3,2,1,0:T(8,128)(2,1)} %pack.87.refs_2_), channel_id=1, source_target_pairs={{2,4},{4,2},{0,1},{6,7},{3,5},{5,3},{1,0},{7,6},{10,12},{12,10},{8... | collective-permute-start | bytes 5505032 | tf_op jit(solution)/shard_map/cond/branch_0_fun/ppermute | solution.py:487
  164.5 66.6 %collective-permute-start.6 = (bf16[3,4,1,32,1792]{4,3,2,1,0:T(8,128)(2,1)}, bf16[3,4,1,32,1792]{4,3,2,1,0:T(8,128)(2,1)}, u32[]{:S(2)}, u32[]{:S(2)}) collective-permute-start(bf16[3,4,1,32,1792]{4,3,2,1,0:T(8,128)(2,1)} %pack.83.refs_1_), channel_id=1, source_target_pairs={{0,1},{2,3},{4,5},{6,7},{1,0},{3,2},{5,4},{7,6},{8,9},{10,11},{12,... | collective-permute-start | bytes 4128776 | tf_op jit(solution)/shard_map/cond/branch_0_fun/ppermute | solution.py:403
  168.7 52.1 %collective-permute-start.8 = (bf16[2,4,1,32,1792]{4,3,2,1,0:T(8,128)(2,1)}, bf16[2,4,1,32,1792]{4,3,2,1,0:T(8,128)(2,1)S(1)}, u32[]{:S(2)}, u32[]{:S(2)}) collective-permute-start(bf16[2,4,1,32,1792]{4,3,2,1,0:T(8,128)(2,1)} %pack.85.refs_2_), channel_id=1, source_target_pairs={{0,2},{2,0},{4,6},{6,4},{1,3},{3,1},{5,7},{7,5},{8,10},{10,8},{12,... | collective-permute-start | bytes 2752520 | tf_op jit(solution)/shard_map/cond/branch_0_fun/ppermute | solution.py:511
  231.2 44.1 %collective-permute-start.11 = (bf16[4,4,1,32,1792]{4,3,2,1,0:T(8,128)(2,1)}, bf16[4,4,1,32,1792]{4,3,2,1,0:T(8,128)(2,1)}, u32[]{:S(2)}, u32[]{:S(2)}) collective-permute-start(bf16[4,4,1,32,1792]{4,3,2,1,0:T(8,128)(2,1)} %copy-done.49), channel_id=1, source_target_pairs={{2,4},{4,2},{0,1},{6,7},{3,5},{5,3},{1,0},{7,6},{10,12},{12,10},{8... | collective-permute-start | bytes 5505032 | tf_op jit(solution)/shard_map/cond/branch_0_fun/ppermute | solution.py:487
  245.3 60.9 %collective-permute-start.9 = (bf16[4,4,1,32,1792]{4,3,2,1,0:T(8,128)(2,1)}, bf16[4,4,1,32,1792]{4,3,2,1,0:T(8,128)(2,1)}, u32[]{:S(2)}, u32[]{:S(2)}) collective-permute-start(bf16[4,4,1,32,1792]{4,3,2,1,0:T(8,128)(2,1)} %pack.94.refs_0_), channel_id=1, source_target_pairs={{0,2},{2,0},{4,6},{6,4},{1,3},{3,1},{5,7},{7,5},{8,10},{10,8},{12,... | collective-permute-start | bytes 5505032 | tf_op jit(solution)/shard_map/cond/branch_0_fun/ppermute | solution.py:511
  251.9 71.6 %collective-permute-start.15 = (bf16[4,4,1,32,1792]{4,3,2,1,0:T(8,128)(2,1)}, bf16[4,4,1,32,1792]{4,3,2,1,0:T(8,128)(2,1)}, u32[]{:S(2)}, u32[]{:S(2)}) collective-permute-start(bf16[4,4,1,32,1792]{4,3,2,1,0:T(8,128)(2,1)} %pack.93.refs_2_), channel_id=1, source_target_pairs={{2,4},{4,2},{0,1},{6,7},{3,5},{5,3},{1,0},{7,6},{10,12},{12,10},{8... | collective-permute-start | bytes 5505032 | tf_op jit(solution)/shard_map/cond/branch_0_fun/ppermute | solution.py:487
  280.8 64.7 %collective-permute-start.21 = (bf16[4,4,1,32,1792]{4,3,2,1,0:T(8,128)(2,1)S(1)}, bf16[4,4,1,32,1792]{4,3,2,1,0:T(8,128)(2,1)S(1)}, u32[]{:S(2)}, u32[]{:S(2)}) collective-permute-start(bf16[4,4,1,32,1792]{4,3,2,1,0:T(8,128)(2,1)S(1)} %pack.97.refs_3_), channel_id=1, source_target_pairs={{0,2},{2,0},{4,6},{6,4},{1,3},{3,1},{5,7},{7,5},{8,10},{10,8},{12,... | collective-permute-start | bytes 5505032 | tf_op jit(solution)/shard_map/cond/branch_0_fun/ppermute | solution.py:511
  280.9 72.9 %collective-permute-start.19 = (bf16[4,4,1,32,1792]{4,3,2,1,0:T(8,128)(2,1)}, bf16[4,4,1,32,1792]{4,3,2,1,0:T(8,128)(2,1)S(1)}, u32[]{:S(2)}, u32[]{:S(2)}) collective-permute-start(bf16[4,4,1,32,1792]{4,3,2,1,0:T(8,128)(2,1)} %pack.96.refs_2_), channel_id=1, source_target_pairs={{2,4},{4,2},{0,1},{6,7},{3,5},{5,3},{1,0},{7,6},{10,12},{12,10},{8... | collective-permute-start | bytes 5505032 | tf_op jit(solution)/shard_map/cond/branch_0_fun/ppermute | solution.py:487
  281.2 53.3 %collective-permute-start.22 = (bf16[3,4,1,32,1792]{4,3,2,1,0:T(8,128)(2,1)}, bf16[3,4,1,32,1792]{4,3,2,1,0:T(8,128)(2,1)}, u32[]{:S(2)}, u32[]{:S(2)}) collective-permute-start(bf16[3,4,1,32,1792]{4,3,2,1,0:T(8,128)(2,1)} %pack.92.refs_1_), channel_id=1, source_target_pairs={{0,1},{2,3},{4,5},{6,7},{1,0},{3,2},{5,4},{7,6},{8,9},{10,11},{12,... | collective-permute-start | bytes 4128776 | tf_op jit(solution)/shard_map/cond/branch_0_fun/ppermute | solution.py:403
  327.5 65.6 %collective-permute-start.16 = (bf16[4,4,1,32,1792]{4,3,2,1,0:T(8,128)(2,1)}, bf16[4,4,1,32,1792]{4,3,2,1,0:T(8,128)(2,1)S(1)}, u32[]{:S(2)}, u32[]{:S(2)}) collective-permute-start(bf16[4,4,1,32,1792]{4,3,2,1,0:T(8,128)(2,1)} %pack.99.refs_2_), channel_id=1, source_target_pairs={{2,4},{4,2},{0,1},{6,7},{3,5},{5,3},{1,0},{7,6},{10,12},{12,10},{8... | collective-permute-start | bytes 5505032 | tf_op jit(solution)/shard_map/cond/branch_0_fun/ppermute | solution.py:487
  359.4 73.0 %collective-permute-start.26 = (bf16[4,4,1,32,1792]{4,3,2,1,0:T(8,128)(2,1)}, bf16[4,4,1,32,1792]{4,3,2,1,0:T(8,128)(2,1)S(1)}, u32[]{:S(2)}, u32[]{:S(2)}) collective-permute-start(bf16[4,4,1,32,1792]{4,3,2,1,0:T(8,128)(2,1)} %pack.102.refs_2_), channel_id=1, source_target_pairs={{2,4},{4,2},{0,1},{6,7},{3,5},{5,3},{1,0},{7,6},{10,12},{12,10},{8... | collective-permute-start | bytes 5505032 | tf_op jit(solution)/shard_map/cond/branch_0_fun/ppermute | solution.py:487
  396.0 75.7 %collective-permute-start.23 = (bf16[4,4,1,32,1792]{4,3,2,1,0:T(8,128)(2,1)}, bf16[4,4,1,32,1792]{4,3,2,1,0:T(8,128)(2,1)S(1)}, u32[]{:S(2)}, u32[]{:S(2)}) collective-permute-start(bf16[4,4,1,32,1792]{4,3,2,1,0:T(8,128)(2,1)} %pack.105.refs_2_), channel_id=1, source_target_pairs={{2,4},{4,2},{0,1},{6,7},{3,5},{5,3},{1,0},{7,6},{10,12},{12,10},{8... | collective-permute-start | bytes 5505032 | tf_op jit(solution)/shard_map/cond/branch_0_fun/ppermute | solution.py:487
  435.5 85.4 %collective-permute-start.30 = (bf16[5,4,1,32,1792]{4,3,2,1,0:T(8,128)(2,1)}, bf16[5,4,1,32,1792]{4,3,2,1,0:T(8,128)(2,1)S(1)}, u32[]{:S(2)}, u32[]{:S(2)}) collective-permute-start(bf16[5,4,1,32,1792]{4,3,2,1,0:T(8,128)(2,1)} %pack.108.refs_2_), channel_id=1, source_target_pairs={{2,4},{4,2},{0,1},{6,7},{3,5},{5,3},{1,0},{7,6},{10,12},{12,10},{8... | collective-permute-start | bytes 6881288 | tf_op jit(solution)/shard_map/cond/branch_0_fun/ppermute | solution.py:487
  474.6 85.7 %collective-permute-start.37 = (bf16[4,4,1,32,1792]{4,3,2,1,0:T(8,128)(2,1)}, bf16[4,4,1,32,1792]{4,3,2,1,0:T(8,128)(2,1)}, u32[]{:S(2)}, u32[]{:S(2)}) collective-permute-start(bf16[4,4,1,32,1792]{4,3,2,1,0:T(8,128)(2,1)} %pack.111.refs_2_), channel_id=1, source_target_pairs={{2,4},{4,2},{0,1},{6,7},{3,5},{5,3},{1,0},{7,6},{10,12},{12,10},{8... | collective-permute-start | bytes 5505032 | tf_op jit(solution)/shard_map/cond/branch_0_fun/ppermute | solution.py:487
  482.4 51.4 %collective-permute-start.28 = (bf16[2,4,1,32,1792]{4,3,2,1,0:T(8,128)(2,1)}, bf16[2,4,1,32,1792]{4,3,2,1,0:T(8,128)(2,1)}, u32[]{:S(2)}, u32[]{:S(2)}) collective-permute-start(bf16[2,4,1,32,1792]{4,3,2,1,0:T(8,128)(2,1)} %pack.112.refs_3_), channel_id=1, source_target_pairs={{0,2},{2,0},{4,6},{6,4},{1,3},{3,1},{5,7},{7,5},{8,10},{10,8},{12,... | collective-permute-start | bytes 2752520 | tf_op jit(solution)/shard_map/cond/branch_0_fun/ppermute | solution.py:511
  524.6 44.5 %collective-permute-start.35 = (bf16[3,4,1,32,1792]{4,3,2,1,0:T(8,128)(2,1)}, bf16[3,4,1,32,1792]{4,3,2,1,0:T(8,128)(2,1)}, u32[]{:S(2)}, u32[]{:S(2)}) collective-permute-start(bf16[3,4,1,32,1792]{4,3,2,1,0:T(8,128)(2,1)} %pack.114.refs_3_), channel_id=1, source_target_pairs={{0,2},{2,0},{4,6},{6,4},{1,3},{3,1},{5,7},{7,5},{8,10},{10,8},{12,... | collective-permute-start | bytes 4128776 | tf_op jit(solution)/shard_map/cond/branch_0_fun/ppermute | solution.py:511
  (75 other events, 963.3 us)
Sparse Core Ops, SparseCore 0:
  10.2 29.0 all-gather.1
  170.5 69.7 all-reduce.3
